TPU v7x, 256 devices: a whole 4x4x8 slice. The times are simulated.
256 devices in a mesh: rows: 32 (over z, x), rhs: 8 (over y, core).
Axes of the slice: x: 4, y: 4, z: 8, core: 2. Of those that a mesh axis runs over, the one named last changes fastest.
Arguments:
- right_side: float32 [32768, 1024], P('rows', 'rhs'), may hold values from -6 to 6
- leaf_blocks: bfloat16 [128, 2, 256, 256], P('rows'), may hold values from -0.25 to 0.25
- out_basis: bfloat16 [128, 2, 256, 128], P('rows'), may hold values from -0.375 to 0.375
- in_basis: bfloat16 [128, 2, 256, 128], P('rows'), may hold values from -0.25 to 0.25
- couplings: bfloat16 [128, 7, 2, 128, 128], P('rows'), may hold values from -6 to 6
Outputs:
- solution: float32 [2, 32768, 1024], P(None, 'rows', 'rhs')
All inputs are finite; a program needn't handle non-finite values.
Results may differ from a plain program's by a relative error of at most 0.0043.
Values sent between devices are 32-bit elements; how exact they have to be, the bound alone decides.
No kernel may reach another device: no remote copies, remote signals or barrier semaphores. Data moves between devices by JAX's collectives and lax.ppermute only.
A program may use at most 64 MiB of HBM per device.

v0:
```python
import math

import jax
import jax.numpy as jnp
from jax import lax
from jax.sharding import PartitionSpec as P


def dft_table(length, phase_sign):
    indices = jnp.arange(length, dtype=jnp.int32)
    product = indices[:, None] * indices[None, :] % length
    angles = 2.0 * math.pi / length * product.astype(jnp.float32)
    return (jnp.cos(angles), phase_sign * jnp.sin(angles))


def exact_mix(pattern, left_re, left_im, right_re, right_im):
    highest = lax.Precision.HIGHEST
    real_part = jnp.einsum(pattern, left_re, right_re, precision=highest) - jnp.einsum(
        pattern, left_im, right_im, precision=highest
    )
    imag_part = jnp.einsum(pattern, left_re, right_im, precision=highest) + jnp.einsum(
        pattern, left_im, right_re, precision=highest
    )
    return (real_part, imag_part)


def narrow_mix(pattern, left_re, left_im, right_re, right_im):
    real_part = jnp.einsum(
        pattern, left_re, right_re, preferred_element_type=jnp.float32
    ) - jnp.einsum(pattern, left_im, right_im, preferred_element_type=jnp.float32)
    imag_part = jnp.einsum(
        pattern, left_re, right_im, preferred_element_type=jnp.float32
    ) + jnp.einsum(pattern, left_im, right_re, preferred_element_type=jnp.float32)
    return (real_part, imag_part)


def local_dft(values_re, values_im, phase_sign):
    length, columns = values_re.shape
    first = 2 ** ((length.bit_length() - 1) // 2)
    second = length // first
    table_re, table_im = dft_table(first, phase_sign)
    grid_re = values_re.reshape(first, second, columns)
    highest = lax.Precision.HIGHEST
    if values_im is None:
        part_re = jnp.einsum("kh,hlc->klc", table_re, grid_re, precision=highest)
        part_im = jnp.einsum("kh,hlc->klc", table_im, grid_re, precision=highest)
    else:
        grid_im = values_im.reshape(first, second, columns)
        part_re, part_im = exact_mix("kh,hlc->klc", table_re, table_im, grid_re, grid_im)
    low_index = jnp.arange(first, dtype=jnp.int32)
    high_index = jnp.arange(second, dtype=jnp.int32)
    twist = (low_index[:, None] * high_index[None, :] % length).astype(jnp.float32) * (
        2.0 * math.pi / length
    )
    twist_re = jnp.cos(twist)[:, :, None]
    twist_im = phase_sign * jnp.sin(twist)[:, :, None]
    turned_re = part_re * twist_re - part_im * twist_im
    turned_im = part_re * twist_im + part_im * twist_re
    outer_re, outer_im = dft_table(second, phase_sign)
    result_re, result_im = exact_mix("jl,klc->jkc", outer_re, outer_im, turned_re, turned_im)
    return (result_re.reshape(length, columns), result_im.reshape(length, columns))


def sibling_sum(values, group):
    count, rank_size, columns = values.shape
    grouped = values.reshape(count // (2 * group), 2, group, rank_size, columns).sum(axis=2)
    swapped = grouped[:, ::-1]
    spread = jnp.broadcast_to(
        swapped[:, :, None], (count // (2 * group), 2, group, rank_size, columns)
    )
    return spread.reshape(count, rank_size, columns)


def shards(right_side, leaf_blocks, out_basis, in_basis, couplings):
    rows_count = lax.axis_size("rows")
    device = lax.axis_index("rows")
    length, columns = right_side.shape
    full_order = length * rows_count
    band_size = length // rows_count
    norm_factor = 1.0 / math.sqrt(full_order)
    positions = jnp.arange(length, dtype=jnp.int32)
    phases = (device * positions % full_order).astype(jnp.float32) * (2.0 * math.pi / full_order)
    phase_re = jnp.cos(phases)[:, None]
    phase_im = jnp.sin(phases)[:, None]
    local_re, local_im = local_dft(right_side, None, -1.0)
    turned = jnp.stack(
        [local_re * phase_re + local_im * phase_im, local_im * phase_re - local_re * phase_im]
    )
    turned = turned.reshape(2, rows_count, band_size, columns)
    across_re, across_im = dft_table(rows_count, -1.0)
    blocks = lax.all_to_all(turned, "rows", split_axis=1, concat_axis=1, tiled=True)
    mixed_re, mixed_im = exact_mix("jd,dqc->jqc", across_re, across_im, blocks[0], blocks[1])
    ordered = (jnp.stack([mixed_re, mixed_im]) * norm_factor).astype(jnp.bfloat16)
    leaf_count = out_basis.shape[0]
    leaf_size = out_basis.shape[2]
    rank_size = out_basis.shape[3]
    level_count = couplings.shape[1]
    inner_levels = leaf_count.bit_length() - 1
    up_levels = rows_count.bit_length() - 1
    leaves = ordered.reshape(2, leaf_count, leaf_size, columns)
    coeff_re, coeff_im = narrow_mix(
        "lar,lac->lrc", in_basis[:, 0], -in_basis[:, 1], leaves[0], leaves[1]
    )
    inner_re = []
    inner_im = []
    for level_index in range(inner_levels):
        group = 2**level_index
        weight = (2.0 * rank_size * level_count * group) ** (-0.5)
        inner_re.append((weight * sibling_sum(coeff_re, group)).astype(jnp.bfloat16))
        inner_im.append((weight * sibling_sum(coeff_im, group)).astype(jnp.bfloat16))
    field_re, field_im = narrow_mix(
        "ltrs,tlsc->lrc",
        couplings[:, :inner_levels, 0],
        couplings[:, :inner_levels, 1],
        jnp.stack(inner_re),
        jnp.stack(inner_im),
    )
    totals = jnp.stack([jnp.sum(coeff_re, axis=0), jnp.sum(coeff_im, axis=0)])
    every = lax.all_gather(totals[None], "rows", axis=0, tiled=True)
    device_ids = jnp.arange(rows_count, dtype=jnp.int32)
    bit_ids = jnp.arange(up_levels, dtype=jnp.int32)
    partner_group = jnp.bitwise_xor(jnp.right_shift(device, bit_ids), 1)
    member = (
        jnp.right_shift(device_ids[None, :], bit_ids[:, None]) == partner_group[:, None]
    ).astype(jnp.float32)
    groups = jnp.einsum("ud,dkrc->ukrc", member, every, precision=lax.Precision.HIGHEST)
    scales = jnp.asarray(
        [
            (2.0 * rank_size * level_count * 2 ** (inner_levels + bit_index)) ** (-0.5)
            for bit_index in range(up_levels)
        ],
        jnp.float32,
    )
    across = (groups * scales[:, None, None, None]).astype(jnp.bfloat16)
    cross_re, cross_im = narrow_mix(
        "lurs,usc->lrc",
        couplings[:, inner_levels:, 0],
        couplings[:, inner_levels:, 1],
        across[:, 0],
        across[:, 1],
    )
    field_low_re = (field_re + cross_re).astype(jnp.bfloat16)
    field_low_im = (field_im + cross_im).astype(jnp.bfloat16)
    far_re, far_im = narrow_mix(
        "lar,lrc->lac", out_basis[:, 0], out_basis[:, 1], field_low_re, field_low_im
    )
    own_re, own_im = narrow_mix(
        "lab,lbc->lac", leaf_blocks[:, 0], leaf_blocks[:, 1], leaves[0], leaves[1]
    )
    image = jnp.stack([own_re + far_re, own_im + far_im])
    image = image.reshape(2, rows_count, band_size, columns)
    back_re, back_im = dft_table(rows_count, 1.0)
    spectral_re, spectral_im = exact_mix("jd,dqc->jqc", back_re, back_im, image[0], image[1])
    blocks = lax.all_to_all(
        jnp.stack([spectral_re, spectral_im]), "rows", split_axis=1, concat_axis=1, tiled=True
    )
    count = blocks.shape[3]
    flat_re = blocks[0].reshape(length, count)
    flat_im = blocks[1].reshape(length, count)
    rolled_re = flat_re * phase_re - flat_im * phase_im
    rolled_im = flat_re * phase_im + flat_im * phase_re
    result_re, result_im = local_dft(rolled_re, rolled_im, 1.0)
    return jnp.stack([result_re, result_im]) * norm_factor


def solution(mesh):
    placed = (
        P("rows", "rhs"),
        P("rows", None, None, None),
        P("rows", None, None, None),
        P("rows", None, None, None),
        P("rows", None, None, None, None),
    )
    return jax.shard_map(
        shards, mesh=mesh, in_specs=placed, out_specs=P(None, "rows", "rhs"), check_vma=False
    )
```

profile of v0, /device:TPU:2, one launch (start us, length us, event | category | flops | bytes accessed | tf_op | source)
XLA Modules:
  0.0 204.1 jit_solution(9726625276925699508)
XLA Ops:
  8.5 1.0 multiply_add_fusion.2
  9.5 0.9 fusion.57
  10.4 0.9 fusion.61
  11.3 0.9 convolution_add_fusion.5
  12.2 1.0 add_bitcast_fusion
  14.0 39.5 %all_to_all.10 = f32[2,32,32,128]{3,2,0,1:T(8,128)S(1)} all-to-all(f32[2,32,32,128]{3,2,0,1:T(8,128)S(1)} %copy.94), channel_id=1, replica_groups=mesh['rows'=32,'rhs'=8] {'rows'}, dimensions={1} | all-to-all | bytes 2097152 | tf_op jit(solution)/shard_map/all_to_all | solution.py:91
  53.5 0.9 fusion.43
  54.4 0.9 fusion.44
  55.3 0.9 fusion.15
  56.2 0.9 fusion.14
  61.0 1.0 convolution_bitcast_fusion.2
  62.0 0.9 convolution_bitcast_fusion.6
  63.6 1.1 convolution_add_fusion.6
  64.7 1.1 convolution_subtract_fusion.6
  65.8 71.9 %all-gather.3.cloned.1.call-done = f32[64,128,128]{2,1,0:T(8,128)} async-done(((f32[2,128,128]{2,1,0:T(8,128)}), f32[64,128,128]{2,1,0:T(8,128)}) %all-gather.3.cloned.1.call-update) | async-done | bytes 4194320 | tf_op jit(solution)/shard_map/all_gather | solution.py:119
  137.7 5.8 %fusion.5 = bf16[5,2,128,128]{3,0,2,1:T(8,128)(2,1)S(1)} fusion(f32[32,2,128,128]{3,2,1,0:T(8,128)} %bitcast.317, f32[5]{0:T(128)S(1)} %copy-done.21, s32[5]{0:T(128)S(1)} %copy-done.22), kind=kOutput, calls=%fused_computation.3 | convolution fusion | flops 63242560 | bytes 4522024 | tf_op jit(solution)/shard_map/ud,dkrc->ukrc/dot_general | solution.py:126
  148.2 0.9 fusion.55
  149.1 0.9 fusion.51
  150.1 0.9 fusion.9
  151.0 0.9 fusion.8
  151.9 1.6 copy.129
  153.5 7.6 %all-to-all-start.1 = ((f32[2,32,32,128]{3,2,0,1:T(8,128)}), f32[2,32,32,128]{3,2,0,1:T(8,128)S(1)}, u32[]{:S(2)}, u32[]{:S(2)}) async-start(f32[2,32,32,128]{3,2,0,1:T(8,128)} %copy.129), calls=%async_computation.1 | async-start | bytes 2097152 | tf_op jit(solution)/shard_map/all_to_all | solution.py:154
  161.3 25.3 %all-to-all-done.1 = f32[2,32,32,128]{3,2,0,1:T(8,128)S(1)} async-done(((f32[2,32,32,128]{3,2,0,1:T(8,128)}), f32[2,32,32,128]{3,2,0,1:T(8,128)S(1)}, u32[]{:S(2)}, u32[]{:S(2)}) %all-to-all-start.1) | async-done | bytes 1048608 | tf_op jit(solution)/shard_map/all_to_all | solution.py:154
  186.6 1.3 fusion.103
  187.9 1.3 fusion.102
  189.2 1.3 convolution_subtract_fusion.1
  190.6 1.4 multiply_subtract_fusion
  192.0 0.9 fusion.49
  192.9 0.9 fusion.45
  193.8 0.9 convolution_subtract_fusion
  194.7 0.9 convolution_add_fusion
  196.2 1.1 maximum_multiply_fusion.1
  (101 shorter events, 12.4 us)
Async XLA Ops:
  6.5 1.0 copy-start
  6.5 131.2 %all-gather.3.cloned.1.call-start = ((), (), s32[]{:S(2)}) async-start(), calls=%async_computation.2 | async-start | bytes 4325376 | tf_op jit(solution)/shard_map/all_gather | solution.py:119
  6.8 3.6 %copy-start.19 = (f32[32,32]{0,1:T(8,128)}, f32[32,32]{0,1:T(8,128)S(1)}, u32[]{:S(2)}) copy-start(f32[32,32]{0,1:T(8,128)S(1)} %copy.85) | copy-start | bytes 12292
  7.6 4.6 %copy-start.7 = (f32[32,32]{0,1:T(8,128)}, f32[32,32]{0,1:T(8,128)S(1)}, u32[]{:S(2)}) copy-start(f32[32,32]{0,1:T(8,128)S(1)} %copy.90) | copy-start | bytes 12292
  57.1 1.0 copy-start.3
  59.0 1.9 copy-start.1
  60.8 2.1 %copy-start.2 = (bf16[4,2,256,256]{3,2,1,0:T(8,128)(2,1)S(1)}, bf16[4,2,256,256]{3,2,1,0:T(8,128)(2,1)}, u32[]{:S(2)}) copy-start(bf16[4,2,256,256]{3,2,1,0:T(8,128)(2,1)} %param.7) | copy-start | bytes 3145732
  60.9 2.3 %copy-start.9 = (bf16[2,2,128,128]{2,3,1,0:T(8,128)(2,1)}, bf16[2,2,128,128]{2,3,1,0:T(8,128)(2,1)S(1)}, u32[]{:S(2)}) copy-start(bf16[2,2,128,128]{2,3,1,0:T(8,128)(2,1)S(1)} %multiply_convert_fusion.1) | copy-start | bytes 393220
  60.9 2.6 %copy-start.11 = (bf16[2,2,128,128]{2,3,1,0:T(8,128)(2,1)}, bf16[2,2,128,128]{2,3,1,0:T(8,128)(2,1)S(1)}, u32[]{:S(2)}) copy-start(bf16[2,2,128,128]{2,3,1,0:T(8,128)(2,1)S(1)} %multiply_convert_fusion) | copy-start | bytes 393220
  61.0 2.6 %copy-start.13 = (bf16[2,2,128,128]{2,3,1,0:T(8,128)(2,1)}, bf16[2,2,128,128]{2,3,1,0:T(8,128)(2,1)S(1)}, u32[]{:S(2)}) copy-start(bf16[2,2,128,128]{2,3,1,0:T(8,128)(2,1)S(1)} %broadcast_in_dim.6) | copy-start | bytes 393220
  62.0 2.7 %copy-start.15 = (bf16[2,2,128,128]{2,3,1,0:T(8,128)(2,1)}, bf16[2,2,128,128]{2,3,1,0:T(8,128)(2,1)S(1)}, u32[]{:S(2)}) copy-start(bf16[2,2,128,128]{2,3,1,0:T(8,128)(2,1)S(1)} %broadcast_in_dim.7) | copy-start | bytes 393220
  63.6 74.2 %copy-start.21 = (f32[5]{0:T(128)S(1)}, f32[5]{0:T(128)}, u32[]{:S(2)}) copy-start(f32[5]{0:T(128)} %constant.88.clone) | copy-start | bytes 64
  63.6 74.2 %copy-start.22 = (s32[5]{0:T(128)S(1)}, s32[5]{0:T(128)}, u32[]{:S(2)}) copy-start(s32[5]{0:T(128)} %shift-right-arithmetic_xor_fusion) | copy-start | bytes 64
  144.4 1.1 copy-start.12
  144.4 1.1 copy-start.16
  144.4 1.1 copy-start.18
  144.8 1.0 copy-start.10
  144.8 1.0 copy-start.14
  144.8 1.1 copy-start.17
  145.2 1.1 copy-start.4
  145.6 1.2 copy-start.6
  146.5 1.1 copy-start.5
  153.5 33.1 %copy-start.8 = (f32[32,32]{0,1:T(8,128)S(1)}, f32[32,32]{0,1:T(8,128)}, u32[]{:S(2)}) copy-start(f32[32,32]{0,1:T(8,128)} %copy-done.7) | copy-start | bytes 12292
  153.5 33.0 %all-to-all-start.1 = ((f32[2,32,32,128]{3,2,0,1:T(8,128)}), f32[2,32,32,128]{3,2,0,1:T(8,128)S(1)}, u32[]{:S(2)}, u32[]{:S(2)}) async-start(f32[2,32,32,128]{3,2,0,1:T(8,128)} %copy.129), calls=%async_computation.1 | async-start | bytes 2097152 | tf_op jit(solution)/shard_map/all_to_all | solution.py:154
  187.9 2.6 %copy-start.20 = (f32[32,32]{0,1:T(8,128)S(1)}, f32[32,32]{0,1:T(8,128)}, u32[]{:S(2)}) copy-start(f32[32,32]{0,1:T(8,128)} %copy-done.19) | copy-start | bytes 12292
Sparse Core Ops, SparseCore 0:
  60.3 77.4 all-gather.2
where the time goes:
time: 205 us; the launch traced here: 204 us
  waiting for transfers between devices  97.2 us (47%)
  blocking collectives  39.5 us (19%)
  matrix products  36.3 us (18%)
  between operations  14.1 us (7%)
  starting transfers between devices  7.6 us (4%)
  local copies, waits for them, and re-layouts  7.04 us (3%)
  other arithmetic  2.41 us (1%)
    all_gather x1, waiting for transfers between devices, shards(): every = lax.all_gather(totals[None], 'rows', axis=0, tiled=True)  71.9 us
    all_to_all x1, blocking collectives, shards(): lax.all_to_all(turned, 'rows', split_axis=1, concat_axis=1, tiled=True)  39.5 us
    all_to_all x1, waiting for transfers between devices, shards(): lax.all_to_all(jnp.stack([spectral_re, spectral_im]), 'rows', split_axis=...  25.3 us
    all_to_all x1, starting transfers between devices, shards(): lax.all_to_all(jnp.stack([spectral_re, spectral_im]), 'rows', split_axis=...  7.6 us
    dot_general x1, matrix products, shards(): jnp.einsum('ud,dkrc->ukrc', member, every, precision=lax.Precision.HIGHEST)  5.82 us
    dot_general x5, matrix products, exact_mix(): jnp.einsum(pattern, left_im, right_re, precision=highest)  5.04 us
    dot_general x5, matrix products, exact_mix(): jnp.einsum(pattern, left_im, right_im, precision=highest)  5.01 us
    dot_general x5, matrix products, exact_mix(): jnp.einsum(pattern, left_re, right_im, precision=highest)  4.87 us
  transfers between devices with their start and end apart: 2, of which 2 were waited for; matrix products, arithmetic and copies ran while one was open for 3% of the time, Pallas kernels for 0%

commit v1 on v0

v1 whole, which is shorter than its diff:
```python
import math

import jax
import jax.numpy as jnp
import ml_dtypes
import numpy as np
from jax import lax
from jax.experimental import pallas as pl
from jax.experimental.pallas import tpu as pltpu
from jax.sharding import PartitionSpec as P

HALF = 128
LANES = 2 * HALF
ROWS = 32
BAND = 32
LENGTH = ROWS * BAND
ORDER = LENGTH * ROWS
NORM = 1.0 / math.sqrt(ORDER)
LEAF = 256
RANK = 128
LEVELS = 7
LEAVES = 4
INNER = 2
UPPER = 5
RADIX = 8
POINTS = LENGTH // RADIX


def split_table(table):
    high = table.astype(ml_dtypes.bfloat16)
    low = (table - high.astype(np.float64)).astype(ml_dtypes.bfloat16)
    return high, low


def forward_tables():
    b = np.arange(RADIX)[:, None, None]
    k = np.arange(POINTS)[None, :, None]
    a = np.arange(POINTS)[None, None, :]
    angle = -2.0 * np.pi * (((8 * a + b) * k) % LENGTH) / LENGTH
    high, low = split_table(np.concatenate([np.cos(angle), np.sin(angle)], 1))
    return np.concatenate([high, low, high], 2)


def inverse_tables():
    b = np.arange(RADIX)[:, None, None]
    a = np.arange(POINTS)[None, :, None]
    k = np.arange(POINTS)[None, None, :]
    angle = 2.0 * np.pi * (((8 * a + b) * k) % LENGTH) / LENGTH
    high, low = split_table(NORM * np.concatenate([np.cos(angle), np.sin(angle)], 2))
    return np.concatenate([high, low, high], 2)


def times_i(x):
    return jnp.concatenate([-x[:, HALF:], x[:, :HALF]], 1)


def packed_fft(values, sign):
    count = len(values)
    if count == 1:
        return values
    even = packed_fft(values[0::2], sign)
    odd = packed_fft(values[1::2], sign)
    half = count // 2
    out = [None] * count
    for k in range(half):
        x = odd[k]
        if k == 0:
            t = x
        elif 4 * k == count:
            t = times_i(x)
            if sign < 0:
                t = -t
        else:
            angle = sign * 2.0 * math.pi * k / count
            t = math.cos(angle) * x + math.sin(angle) * times_i(x)
        out[k] = even[k] + t
        out[k + half] = even[k] - t
    return out


def split_fft(values, sign):
    count = len(values)
    if count == 1:
        return values
    even = split_fft(values[0::2], sign)
    odd = split_fft(values[1::2], sign)
    half = count // 2
    out = [None] * count
    for k in range(half):
        re, im = odd[k]
        if k == 0:
            t = (re, im)
        elif 4 * k == count:
            t = (-im, re) if sign > 0 else (im, -re)
        else:
            c = math.cos(2.0 * math.pi * k / count)
            s = sign * math.sin(2.0 * math.pi * k / count)
            t = (c * re - s * im, c * im + s * re)
        e = even[k]
        out[k] = (e[0] + t[0], e[1] + t[1])
        out[k + half] = (e[0] - t[0], e[1] - t[1])
    return out


def small_phase(x):
    y = x * x
    c = 1.0 + y * (-1.0 / 2 + y * (1.0 / 24 + y * (-1.0 / 720 + y * (1.0 / 40320 - y / 3628800.0))))
    s = x * (1.0 + y * (-1.0 / 6 + y * (1.0 / 120 + y * (-1.0 / 5040 + y * (1.0 / 362880 - y / 39916800.0)))))
    return c, s


def cmul(x, y):
    return (x[0] * y[0] - x[1] * y[1], x[0] * y[1] + x[1] * y[0])


def block_phases(device, sign):
    shape = (8, HALF)
    step = jnp.full(shape, 1.0, jnp.float32) * (device.astype(jnp.float32) * (sign * 2.0 * math.pi / 256.0))
    one = small_phase(step)
    two = cmul(one, one)
    four = cmul(two, two)
    three = cmul(two, one)
    return [None, one, two, three, four, cmul(four, one), cmul(four, two), cmul(four, three)]


def row_phase(device, start, sign):
    row = (lax.broadcasted_iota(jnp.int32, (8, HALF), 0) + start).astype(jnp.float32)
    return small_phase(row * (device.astype(jnp.float32) * (sign * 2.0 * math.pi / ORDER)))


def forward_kernel(x_ref, table_ref, out_ref, part_ref):
    device = lax.axis_index("rows")
    for b in range(RADIX):
        x = x_ref[pl.ds(b, POINTS, stride=RADIX), :]
        high = x.astype(jnp.bfloat16)
        low = (x - high.astype(jnp.float32)).astype(jnp.bfloat16)
        part_ref[b] = jnp.dot(
            table_ref[b], jnp.concatenate([high, high, low], 0), preferred_element_type=jnp.float32
        )
    blocks = block_phases(device, -1.0)
    for g in range(POINTS // 8):
        rows = row_phase(device, 8 * g, -1.0)
        values = [
            (part_ref[b, 8 * g : 8 * g + 8, :], part_ref[b, POINTS + 8 * g : POINTS + 8 * g + 8, :])
            for b in range(RADIX)
        ]
        values = split_fft(values, -1)
        for k in range(RADIX):
            phase = rows if k == 0 else cmul(rows, blocks[k])
            re, im = cmul(values[k], phase)
            at = POINTS * k + 8 * g
            out_ref[at // BAND, at % BAND : at % BAND + 8, :HALF] = re
            out_ref[at // BAND, at % BAND : at % BAND + 8, HALF:] = im


def forward_call(x):
    shape = jax.ShapeDtypeStruct((ROWS, BAND, LANES), jnp.float32)
    table = jnp.asarray(forward_tables())
    vmem = pl.BlockSpec(memory_space=pltpu.VMEM)
    return pl.pallas_call(
        forward_kernel,
        out_shape=shape,
        in_specs=[vmem, vmem],
        out_specs=vmem,
        scratch_shapes=[pltpu.VMEM((RADIX, 2 * POINTS, HALF), jnp.float32)],
        compiler_params=pltpu.CompilerParams(vmem_limit_bytes=16 * 2**20),
        cost_estimate=pl.CostEstimate(flops=3 * 10**8, bytes_accessed=3 * 2**20, transcendentals=0),
        name="local_forward",
    )(x, table)


def transposed_dot(left, right):
    return lax.dot_general(left, right, (((0,), (0,)), ((), ())), preferred_element_type=jnp.float32)


def coefficient_kernel(block_ref, basis_ref, ordered_ref, coeff_ref, total_ref, scratch_ref):
    for g in range(BAND // 8):
        values = packed_fft([block_ref[d, 8 * g : 8 * g + 8, :] for d in range(ROWS)], -1)
        for j in range(ROWS):
            scratch_ref[BAND * j + 8 * g : BAND * j + 8 * g + 8, :] = NORM * values[j]
    total = None
    for leaf in range(LEAVES):
        x = scratch_ref[LEAF * leaf : LEAF * (leaf + 1), :]
        rounded = x.astype(jnp.bfloat16)
        turned = times_i(x).astype(jnp.bfloat16)
        ordered_ref[leaf, :LEAF, :] = rounded
        ordered_ref[leaf, LEAF:, :] = turned
        coeff = transposed_dot(basis_ref[leaf, 0], rounded) - transposed_dot(basis_ref[leaf, 1], turned)
        coeff_ref[leaf] = coeff
        total = coeff if total is None else total + coeff
    total_ref[...] = total


def coefficient_call(block, in_basis):
    vmem = pl.BlockSpec(memory_space=pltpu.VMEM)
    return pl.pallas_call(
        coefficient_kernel,
        out_shape=(
            jax.ShapeDtypeStruct((LEAVES, 2 * LEAF, LANES), jnp.bfloat16),
            jax.ShapeDtypeStruct((LEAVES, RANK, LANES), jnp.float32),
            jax.ShapeDtypeStruct((RANK, LANES), jnp.float32),
        ),
        in_specs=[vmem] * 2,
        out_specs=(vmem,) * 3,
        scratch_shapes=[pltpu.VMEM((LENGTH, LANES), jnp.float32)],
        compiler_params=pltpu.CompilerParams(vmem_limit_bytes=16 * 2**20),
        cost_estimate=pl.CostEstimate(flops=10**8, bytes_accessed=2 * 2**20, transcendentals=0),
        name="coefficients",
    )(block, in_basis)


def scale_of(level):
    return (2.0 * RANK * LEVELS * 2**level) ** (-0.5)


def with_turned(x):
    return [x.astype(jnp.bfloat16), times_i(x).astype(jnp.bfloat16)]


def near_kernel(ordered_ref, coeff_ref, blocks_ref, couplings_ref, own_ref, near_ref):
    for leaf in range(LEAVES):
        matrix = jnp.concatenate([blocks_ref[leaf, 0], blocks_ref[leaf, 1]], 1)
        own_ref[leaf] = jnp.dot(matrix, ordered_ref[leaf], preferred_element_type=jnp.float32)
        other = 2 * (1 - leaf // 2)
        siblings = with_turned(scale_of(0) * coeff_ref[leaf ^ 1]) + with_turned(
            scale_of(1) * (coeff_ref[other] + coeff_ref[other + 1])
        )
        matrix = jnp.concatenate([couplings_ref[leaf, t, part] for t in range(INNER) for part in range(2)], 1)
        near_ref[leaf] = jnp.dot(matrix, jnp.concatenate(siblings, 0), preferred_element_type=jnp.float32)


def near_call(ordered, coeff, leaf_blocks, couplings):
    vmem = pl.BlockSpec(memory_space=pltpu.VMEM)
    return pl.pallas_call(
        near_kernel,
        out_shape=(
            jax.ShapeDtypeStruct((LEAVES, LEAF, LANES), jnp.float32),
            jax.ShapeDtypeStruct((LEAVES, RANK, LANES), jnp.float32),
        ),
        in_specs=[vmem] * 4,
        out_specs=(vmem,) * 2,
        compiler_params=pltpu.CompilerParams(vmem_limit_bytes=16 * 2**20),
        cost_estimate=pl.CostEstimate(flops=2 * 10**8, bytes_accessed=4 * 2**20, transcendentals=0),
        name="near_field",
    )(ordered, coeff, leaf_blocks, couplings)


def image_kernel(own_ref, near_ref, couplings_ref, basis_ref, *refs):
    sibling_refs, out_ref, scratch_ref = refs[:UPPER], refs[UPPER], refs[UPPER + 1]
    siblings = []
    for level in range(UPPER):
        siblings += with_turned(scale_of(INNER + level) * sibling_refs[level][...])
    siblings = jnp.concatenate(siblings, 0)
    for leaf in range(LEAVES):
        matrix = jnp.concatenate(
            [couplings_ref[leaf, INNER + level, part] for level in range(UPPER) for part in range(2)], 1
        )
        field = near_ref[leaf] + jnp.dot(matrix, siblings, preferred_element_type=jnp.float32)
        matrix = jnp.concatenate([basis_ref[leaf, 0], basis_ref[leaf, 1]], 1)
        scratch_ref[LEAF * leaf : LEAF * (leaf + 1), :] = own_ref[leaf] + jnp.dot(
            matrix, jnp.concatenate(with_turned(field), 0), preferred_element_type=jnp.float32
        )
    for g in range(BAND // 8):
        values = packed_fft(
            [scratch_ref[BAND * j + 8 * g : BAND * j + 8 * g + 8, :] for j in range(ROWS)], 1
        )
        for d in range(ROWS):
            out_ref[d, 8 * g : 8 * g + 8, :] = values[d]


def image_call(own, near, couplings, out_basis, siblings):
    vmem = pl.BlockSpec(memory_space=pltpu.VMEM)
    return pl.pallas_call(
        image_kernel,
        out_shape=jax.ShapeDtypeStruct((ROWS, BAND, LANES), jnp.float32),
        in_specs=[vmem] * (4 + UPPER),
        out_specs=vmem,
        scratch_shapes=[pltpu.VMEM((LENGTH, LANES), jnp.float32)],
        compiler_params=pltpu.CompilerParams(vmem_limit_bytes=16 * 2**20),
        cost_estimate=pl.CostEstimate(flops=3 * 10**8, bytes_accessed=4 * 2**20, transcendentals=0),
        name="image",
    )(own, near, couplings, out_basis, *siblings)


def inverse_kernel(block_ref, table_ref, out_ref, turned_ref):
    device = lax.axis_index("rows")
    blocks = block_phases(device, 1.0)
    for g in range(POINTS // 8):
        rows = row_phase(device, 8 * g, 1.0)
        values = []
        for k in range(RADIX):
            phase = rows if k == 0 else cmul(rows, blocks[k])
            at = POINTS * k + 8 * g
            x = block_ref[at // BAND, at % BAND : at % BAND + 8, :]
            values.append(jnp.concatenate(cmul((x[:, :HALF], x[:, HALF:]), phase), 1))
        values = packed_fft(values, 1)
        for b in range(RADIX):
            turned_ref[b, 8 * g : 8 * g + 8, :] = values[b]
    for b in range(RADIX):
        x = turned_ref[b]
        high = x.astype(jnp.bfloat16)
        low = (x - high.astype(jnp.float32)).astype(jnp.bfloat16)
        high_y, low_y = times_i(high), times_i(low)
        value = jnp.dot(
            table_ref[b],
            jnp.concatenate([high, high_y, high, high_y, low, low_y], 0),
            preferred_element_type=jnp.float32,
        )
        out_ref[0, pl.ds(b, POINTS, stride=RADIX), :] = value[:, :HALF]
        out_ref[1, pl.ds(b, POINTS, stride=RADIX), :] = value[:, HALF:]


def inverse_call(block):
    vmem = pl.BlockSpec(memory_space=pltpu.VMEM)
    table = jnp.asarray(inverse_tables())
    return pl.pallas_call(
        inverse_kernel,
        out_shape=jax.ShapeDtypeStruct((2, LENGTH, HALF), jnp.float32),
        in_specs=[vmem] * 2,
        out_specs=vmem,
        scratch_shapes=[pltpu.VMEM((RADIX, POINTS, LANES), jnp.float32)],
        compiler_params=pltpu.CompilerParams(vmem_limit_bytes=16 * 2**20),
        cost_estimate=pl.CostEstimate(flops=3 * 10**8, bytes_accessed=3 * 2**20, transcendentals=0),
        name="local_inverse",
    )(block, table)


def exchange(total):
    held, siblings = total, []
    for bit in range(UPPER):
        pairs = [(i, i ^ (1 << bit)) for i in range(ROWS)]
        siblings.append(lax.ppermute(held, "rows", pairs))
        held = held + siblings[-1]
    return siblings


def swap_blocks(block):
    return lax.all_to_all(block, "rows", split_axis=0, concat_axis=0, tiled=True)


def shards(right_side, leaf_blocks, out_basis, in_basis, couplings):
    block = swap_blocks(forward_call(right_side))
    ordered, coeff, total = coefficient_call(block, in_basis)
    siblings = exchange(total)
    own, near = near_call(ordered, coeff, leaf_blocks, couplings)
    return inverse_call(swap_blocks(image_call(own, near, couplings, out_basis, siblings)))


def solution(mesh):
    placed = (
        P("rows", "rhs"),
        P("rows", None, None, None),
        P("rows", None, None, None),
        P("rows", None, None, None),
        P("rows", None, None, None, None),
    )
    return jax.shard_map(
        shards, mesh=mesh, in_specs=placed, out_specs=P(None, "rows", "rhs"), check_vma=False
    )
```

time: 205 us -> 110 us (0.54)
  waiting for transfers between devices: 97.2 us -> 29.4 us
  matrix products: 36.3 us -> 0 us
  blocking collectives: 39.5 us -> 66.4 us
  between operations: 14.1 us -> 0.07 us
  Pallas kernels: 0 us -> 6.01 us
  local copies, waits for them, and re-layouts: 7.04 us -> 2.47 us
  other arithmetic: 2.41 us -> 0.07 us
    all_gather x1 -> x0, waiting for transfers between devices: 71.9 us -> none  [shards(): every = lax.all_gather(totals[None], 'rows', axis=0, tiled=True)]
    dot_general x43 -> x0, matrix products: 36.3 us -> none  [the longest x1 5.82 us: shards(): jnp.einsum('ud,dkrc->ukrc', member, every, precision=lax.Precision.HIGHEST)]
    ppermute x0 -> x5, waiting for transfers between devices: none -> 29.4 us  [exchange(): siblings.append(lax.ppermute(held, 'rows', pairs))]
    all_to_all x1 -> x2, blocking collectives: 39.5 us -> 66.4 us  [swap_blocks(): lax.all_to_all(block, 'rows', split_axis=0, concat_axis=0, tiled=True)]
    all_to_all x1 -> x0, waiting for transfers between devices: 25.3 us -> none  [shards(): lax.all_to_all(jnp.stack([spectral_re, spectral_im]), 'rows', split_axis=...]
    all_to_all x1 -> x0, starting transfers between devices: 7.6 us -> none  [shards(): lax.all_to_all(jnp.stack([spectral_re, spectral_im]), 'rows', split_axis=...]
    pallas_call x0 -> x5, Pallas kernels: none -> 6.01 us  [the longest x1 1.95 us: inverse_call(): pl.pallas_call(inverse_kernel, out_shape=jax.ShapeDtypeStruct((2, LENGTH,...]
    ppermute x0 -> x5, starting transfers between devices: none -> 5.69 us  [exchange(): siblings.append(lax.ppermute(held, 'rows', pairs))]
  transfers between devices with their start and end apart: 2 -> 5, of which waited for: 2 -> 5; matrix products, arithmetic and copies ran while one was open for 3% -> 0% of each run, Pallas kernels for 0% -> 1%
where the time goes in v1:
time: 110 us
  blocking collectives  66.4 us (60%)
  waiting for transfers between devices  29.4 us (27%)
  Pallas kernels  6.01 us (5%)
  starting transfers between devices  5.69 us (5%)
  local copies, waits for them, and re-layouts  2.47 us (2%)
    all_to_all x2, blocking collectives, swap_blocks(): lax.all_to_all(block, 'rows', split_axis=0, concat_axis=0, tiled=True)  66.4 us
    ppermute x5, waiting for transfers between devices, exchange(): siblings.append(lax.ppermute(held, 'rows', pairs))  29.4 us
    ppermute x5, starting transfers between devices, exchange(): siblings.append(lax.ppermute(held, 'rows', pairs))  5.69 us
    unnamed x14, local copies, waits for them, and re-layouts  2.47 us
  transfers between devices with their start and end apart: 5, of which 5 were waited for; matrix products, arithmetic and copies ran while one was open for 0% of the time, Pallas kernels for 1%

profile of v1, /device:TPU:2, one launch (start us, length us, event | category | flops | bytes accessed | tf_op | source)
XLA Modules:
  0.0 110.1 jit_solution(8763630007567729965)
XLA Ops:
  0.0 0.0 copy-start.2
  0.0 1.4 %copy-done.2 = bf16[8,256,384]{2,1,0:T(8,128)(2,1)S(1)} copy-done((bf16[8,256,384]{2,1,0:T(8,128)(2,1)S(1)}, bf16[8,256,384]{2,1,0:T(8,128)(2,1)}, u32[]{:S(2)}) %copy-start.2) | copy-done | bytes 1572888
  1.4 0.0 copy-start.5
  1.4 1.0 copy-done.5
  2.5 0.9 local_forward.1
  3.3 0.0 copy-start.4
  3.4 39.6 %all_to_all.10.block_ref = f32[32,32,256]{2,1,0:T(8,128)S(1)} all-to-all(f32[32,32,256]{2,1,0:T(8,128)S(1)} %local_forward.1), channel_id=1, replica_groups=mesh['rows'=32,'rhs'=8] {'rows'}, dimensions={0} | all-to-all | bytes 2097152 | tf_op jit(solution)/shard_map/all_to_all | solution.py:338
  43.0 0.0 copy-done.4
  43.0 0.0 copy-start
  43.0 0.0 copy-start.3
  43.0 0.7 coefficients.1
  43.7 0.3 collective-permute-start
  44.0 4.7 %collective-permute-done.refs_0_ = f32[128,256]{1,0:T(8,128)S(1)} collective-permute-done((f32[128,256]{1,0:T(8,128)S(1)}, f32[128,256]{1,0:T(8,128)S(1)}, u32[]{:S(2)}, u32[]{:S(2)}) %collective-permute-start) | collective-permute-done | bytes 131104 | tf_op jit(solution)/shard_map/ppermute | solution.py:332
  48.8 3.3 %collective-permute-start.1 = (f32[128,256]{1,0:T(8,128)S(1)}, f32[128,256]{1,0:T(8,128)S(1)}, u32[]{:S(2)}, u32[]{:S(2)}) collective-permute-start(f32[128,256]{1,0:T(8,128)S(1)} %add.12), channel_id=1, source_target_pairs={{0,16},{8,24},{16,0},{24,8},{32,48},{40,56},{48,32},{56,40},{64,80... | collective-permute-start | bytes 393224 | tf_op jit(solution)/shard_map/ppermute | solution.py:332
  52.1 3.2 %collective-permute-done.1.refs_1_ = f32[128,256]{1,0:T(8,128)S(1)} collective-permute-done((f32[128,256]{1,0:T(8,128)S(1)}, f32[128,256]{1,0:T(8,128)S(1)}, u32[]{:S(2)}, u32[]{:S(2)}) %collective-permute-start.1) | collective-permute-done | bytes 131104 | tf_op jit(solution)/shard_map/ppermute | solution.py:332
  55.3 0.7 collective-permute-start.2
  56.0 5.7 %collective-permute-done.2.refs_2_ = f32[128,256]{1,0:T(8,128)S(1)} collective-permute-done((f32[128,256]{1,0:T(8,128)S(1)}, f32[128,256]{1,0:T(8,128)S(1)}, u32[]{:S(2)}, u32[]{:S(2)}) %collective-permute-start.2) | collective-permute-done | bytes 131104 | tf_op jit(solution)/shard_map/ppermute | solution.py:332
  61.7 0.5 collective-permute-start.3
  62.2 8.3 %collective-permute-done.3.refs_3_ = f32[128,256]{1,0:T(8,128)S(1)} collective-permute-done((f32[128,256]{1,0:T(8,128)S(1)}, f32[128,256]{1,0:T(8,128)S(1)}, u32[]{:S(2)}, u32[]{:S(2)}) %collective-permute-start.3) | collective-permute-done | bytes 131104 | tf_op jit(solution)/shard_map/ppermute | solution.py:332
  70.5 0.8 collective-permute-start.4
  71.4 0.0 copy-done
  71.4 0.0 copy-done.3
  71.4 0.0 copy-start.6
  71.4 0.6 near_field.1
  71.9 7.5 %collective-permute-done.4.refs_4_ = f32[128,256]{1,0:T(8,128)S(1)} collective-permute-done((f32[128,256]{1,0:T(8,128)S(1)}, f32[128,256]{1,0:T(8,128)S(1)}, u32[]{:S(2)}, u32[]{:S(2)}) %collective-permute-start.4) | collective-permute-done | bytes 131104 | tf_op jit(solution)/shard_map/ppermute | solution.py:332
  79.5 0.0 copy-done.6
  79.5 1.9 %image.1 = f32[32,32,256]{2,1,0:T(8,128)S(1)} custom-call(f32[4,256,256]{2,1,0:T(8,128)S(1)} %get-tuple-element.12.own_ref, f32[4,128,256]{2,1,0:T(8,128)S(1)} %get-tuple-element.13.near_ref, bf16[4,7,2,128,128]{4,3,2,1,0:T(8,128)(2,1)S(1)} %copy-done, bf16[4,2,256,128]{3,2,1,0:T(8,128)(2,1)S(1)} %copy-done.6, f32[128,256]{1,0:T(8,128)S(1)} %collective-permute-done.refs_0_, ...), custom_call_target="tpu_custom_call" | custom-call | flops 300000000 | bytes 4194304 | tf_op jit(solution)/shard_map/image/pallas_call | solution.py:273
  81.4 0.0 copy-start.1
  81.4 26.8 %all_to_all.11.block_ref = f32[32,32,256]{2,1,0:T(8,128)S(1)} all-to-all(f32[32,32,256]{2,1,0:T(8,128)S(1)} %image.1), channel_id=1, replica_groups=mesh['rows'=32,'rhs'=8] {'rows'}, dimensions={0} | all-to-all | bytes 2097152 | tf_op jit(solution)/shard_map/all_to_all | solution.py:338
  108.2 0.0 copy-done.1
  108.2 2.0 %local_inverse.1 = f32[2,1024,128]{2,1,0:T(8,128)} custom-call(f32[32,32,256]{2,1,0:T(8,128)S(1)} %all_to_all.11.block_ref, bf16[8,128,768]{2,1,0:T(8,128)(2,1)S(1)} %copy-done.1), custom_call_target="tpu_custom_call" | custom-call | flops 300000000 | bytes 3145728 | tf_op jit(solution)/shard_map/local_inverse/pallas_call | solution.py:316
  (4 shorter events, 0.1 us)
Async XLA Ops:
  0.0 1.4 %copy-start.2 = (bf16[8,256,384]{2,1,0:T(8,128)(2,1)S(1)}, bf16[8,256,384]{2,1,0:T(8,128)(2,1)}, u32[]{:S(2)}) copy-start(bf16[8,256,384]{2,1,0:T(8,128)(2,1)} %constant.4.clone.table_ref) | copy-start | bytes 4718596
  1.4 1.0 copy-start.5
  3.3 39.6 %copy-start.4 = (bf16[4,2,256,128]{3,2,1,0:T(8,128)(2,1)S(1)}, bf16[4,2,256,128]{3,2,1,0:T(8,128)(2,1)}, u32[]{:S(2)}) copy-start(bf16[4,2,256,128]{3,2,1,0:T(8,128)(2,1)} %basis_ref.2) | copy-start | bytes 1572868
  43.0 28.4 %copy-start = (bf16[4,7,2,128,128]{4,3,2,1,0:T(8,128)(2,1)S(1)}, bf16[4,7,2,128,128]{4,3,2,1,0:T(8,128)(2,1)}, u32[]{:S(2)}) copy-start(bf16[4,7,2,128,128]{4,3,2,1,0:T(8,128)(2,1)} %couplings_ref.3) | copy-start | bytes 5505028
  43.0 28.4 %copy-start.3 = (bf16[4,2,256,256]{3,2,1,0:T(8,128)(2,1)S(1)}, bf16[4,2,256,256]{3,2,1,0:T(8,128)(2,1)}, u32[]{:S(2)}) copy-start(bf16[4,2,256,256]{3,2,1,0:T(8,128)(2,1)} %blocks_ref.1) | copy-start | bytes 3145732
  43.7 5.1 %collective-permute-start = (f32[128,256]{1,0:T(8,128)S(1)}, f32[128,256]{1,0:T(8,128)S(1)}, u32[]{:S(2)}, u32[]{:S(2)}) collective-permute-start(f32[128,256]{1,0:T(8,128)S(1)} %get-tuple-element.14), channel_id=1, source_target_pairs={{0,8},{8,0},{16,24},{24,16},{32,40},{40,32},{48,56},{56,48},{64,72... | collective-permute-start | bytes 393224 | tf_op jit(solution)/shard_map/ppermute | solution.py:332
  48.8 6.6 %collective-permute-start.1 = (f32[128,256]{1,0:T(8,128)S(1)}, f32[128,256]{1,0:T(8,128)S(1)}, u32[]{:S(2)}, u32[]{:S(2)}) collective-permute-start(f32[128,256]{1,0:T(8,128)S(1)} %add.12), channel_id=1, source_target_pairs={{0,16},{8,24},{16,0},{24,8},{32,48},{40,56},{48,32},{56,40},{64,80... | collective-permute-start | bytes 393224 | tf_op jit(solution)/shard_map/ppermute | solution.py:332
  55.3 6.3 %collective-permute-start.2 = (f32[128,256]{1,0:T(8,128)S(1)}, f32[128,256]{1,0:T(8,128)S(1)}, u32[]{:S(2)}, u32[]{:S(2)}) collective-permute-start(f32[128,256]{1,0:T(8,128)S(1)} %add.13), channel_id=1, source_target_pairs={{0,32},{8,40},{16,48},{24,56},{32,0},{40,8},{48,16},{56,24},{64,96... | collective-permute-start | bytes 393224 | tf_op jit(solution)/shard_map/ppermute | solution.py:332
  61.7 8.8 %collective-permute-start.3 = (f32[128,256]{1,0:T(8,128)S(1)}, f32[128,256]{1,0:T(8,128)S(1)}, u32[]{:S(2)}, u32[]{:S(2)}) collective-permute-start(f32[128,256]{1,0:T(8,128)S(1)} %add.14), channel_id=1, source_target_pairs={{0,64},{8,72},{16,80},{24,88},{32,96},{40,104},{48,112},{56,120},{... | collective-permute-start | bytes 393224 | tf_op jit(solution)/shard_map/ppermute | solution.py:332
  70.5 9.0 %collective-permute-start.4 = (f32[128,256]{1,0:T(8,128)S(1)}, f32[128,256]{1,0:T(8,128)S(1)}, u32[]{:S(2)}, u32[]{:S(2)}) collective-permute-start(f32[128,256]{1,0:T(8,128)S(1)} %add.15), channel_id=1, source_target_pairs={{0,128},{8,136},{16,144},{24,152},{32,160},{40,168},{48,176},{56,1... | collective-permute-start | bytes 393224 | tf_op jit(solution)/shard_map/ppermute | solution.py:332
  71.4 8.1 %copy-start.6 = (bf16[4,2,256,128]{3,2,1,0:T(8,128)(2,1)S(1)}, bf16[4,2,256,128]{3,2,1,0:T(8,128)(2,1)}, u32[]{:S(2)}) copy-start(bf16[4,2,256,128]{3,2,1,0:T(8,128)(2,1)} %basis_ref.3) | copy-start | bytes 1572868
  81.4 26.8 %copy-start.1 = (bf16[8,128,768]{2,1,0:T(8,128)(2,1)S(1)}, bf16[8,128,768]{2,1,0:T(8,128)(2,1)}, u32[]{:S(2)}) copy-start(bf16[8,128,768]{2,1,0:T(8,128)(2,1)} %constant.5.clone.table_ref) | copy-start | bytes 4718596

commit v2 on v1

--- a/solution.py
+++ b/solution.py
@@ -22,6 +22,7 @@
 LEAVES = 4
 INNER = 2
 UPPER = 5
+EARLY = 4
 RADIX = 8
 POINTS = LENGTH // RADIX
 
@@ -32,13 +33,12 @@
     return high, low
 
 
-def forward_tables():
-    b = np.arange(RADIX)[:, None, None]
-    k = np.arange(POINTS)[None, :, None]
-    a = np.arange(POINTS)[None, None, :]
-    angle = -2.0 * np.pi * (((8 * a + b) * k) % LENGTH) / LENGTH
-    high, low = split_table(np.concatenate([np.cos(angle), np.sin(angle)], 1))
-    return np.concatenate([high, low, high], 2)
+def forward_table():
+    k = np.arange(POINTS)[:, None]
+    a = np.arange(POINTS)[None, :]
+    angle = -2.0 * np.pi * ((a * k) % POINTS) / POINTS
+    high, low = split_table(np.concatenate([np.cos(angle), np.sin(angle)], 0))
+    return np.concatenate([high, low, high], 1)
 
 
 def inverse_tables():
@@ -78,6 +78,21 @@
     return out
 
 
+def across(load, store, hold_ref, sign):
+    for b in range(4):
+        values = packed_fft([load(4 * a + b) for a in range(8)], sign)
+        for c in range(8):
+            x = values[c]
+            if b and c:
+                angle = sign * 2.0 * math.pi * b * c / 32
+                x = math.cos(angle) * x + math.sin(angle) * times_i(x)
+            hold_ref[b, 8 * c : 8 * c + 8, :] = x
+    for c in range(8):
+        values = packed_fft([hold_ref[b, 8 * c : 8 * c + 8, :] for b in range(4)], sign)
+        for d in range(4):
+            store(c + 8 * d, values[d])
+
+
 def split_fft(values, sign):
     count = len(values)
     if count == 1:
@@ -125,59 +140,67 @@
 
 def row_phase(device, start, sign):
     row = (lax.broadcasted_iota(jnp.int32, (8, HALF), 0) + start).astype(jnp.float32)
-    return small_phase(row * (device.astype(jnp.float32) * (sign * 2.0 * math.pi / ORDER)))
-
-
-def forward_kernel(x_ref, table_ref, out_ref, part_ref):
+    scale = sign * 2.0 * math.pi / ORDER
+    return small_phase(row * (device * scale if isinstance(device, int) else device.astype(jnp.float32) * scale))
+
+
+def forward_kernel(x_ref, table_ref, turn_ref, out_ref, part_ref):
     device = lax.axis_index("rows")
-    for b in range(RADIX):
-        x = x_ref[pl.ds(b, POINTS, stride=RADIX), :]
+    table = table_ref[...]
+    for pair in range(RADIX // 2):
+        x = jnp.concatenate([x_ref[pl.ds(2 * pair + i, POINTS, stride=RADIX), :] for i in range(2)], 1)
         high = x.astype(jnp.bfloat16)
         low = (x - high.astype(jnp.float32)).astype(jnp.bfloat16)
-        part_ref[b] = jnp.dot(
-            table_ref[b], jnp.concatenate([high, high, low], 0), preferred_element_type=jnp.float32
-        )
+        part = jnp.dot(table, jnp.concatenate([high, high, low], 0), preferred_element_type=jnp.float32)
+        part_ref[2 * pair] = part[:, :HALF]
+        part_ref[2 * pair + 1] = part[:, HALF:]
     blocks = block_phases(device, -1.0)
     for g in range(POINTS // 8):
-        rows = row_phase(device, 8 * g, -1.0)
-        values = [
-            (part_ref[b, 8 * g : 8 * g + 8, :], part_ref[b, POINTS + 8 * g : POINTS + 8 * g + 8, :])
-            for b in range(RADIX)
-        ]
+        step = row_phase(32, 8 * g, -1.0)
+        turn = row_phase(device, 8 * g, -1.0)
+        values = []
+        for b in range(RADIX):
+            turn = turn if b == 0 else cmul(turn, step)
+            part = (part_ref[b, 8 * g : 8 * g + 8, :], part_ref[b, POINTS + 8 * g : POINTS + 8 * g + 8, :])
+            values.append(cmul(part, turn))
         values = split_fft(values, -1)
         for k in range(RADIX):
-            phase = rows if k == 0 else cmul(rows, blocks[k])
-            re, im = cmul(values[k], phase)
+            re, im = values[k] if k == 0 else cmul(values[k], blocks[k])
             at = POINTS * k + 8 * g
             out_ref[at // BAND, at % BAND : at % BAND + 8, :HALF] = re
             out_ref[at // BAND, at % BAND : at % BAND + 8, HALF:] = im
 
 
-def forward_call(x):
+def forward_call(x, turn):
     shape = jax.ShapeDtypeStruct((ROWS, BAND, LANES), jnp.float32)
-    table = jnp.asarray(forward_tables())
+    table = jnp.asarray(forward_table())
     vmem = pl.BlockSpec(memory_space=pltpu.VMEM)
     return pl.pallas_call(
         forward_kernel,
         out_shape=shape,
-        in_specs=[vmem, vmem],
+        in_specs=[vmem, vmem, pl.BlockSpec(memory_space=pl.ANY)],
         out_specs=vmem,
         scratch_shapes=[pltpu.VMEM((RADIX, 2 * POINTS, HALF), jnp.float32)],
         compiler_params=pltpu.CompilerParams(vmem_limit_bytes=16 * 2**20),
         cost_estimate=pl.CostEstimate(flops=3 * 10**8, bytes_accessed=3 * 2**20, transcendentals=0),
         name="local_forward",
-    )(x, table)
+    )(x, table, turn)
 
 
 def transposed_dot(left, right):
     return lax.dot_general(left, right, (((0,), (0,)), ((), ())), preferred_element_type=jnp.float32)
 
 
-def coefficient_kernel(block_ref, basis_ref, ordered_ref, coeff_ref, total_ref, scratch_ref):
+def coefficient_kernel(block_ref, basis_ref, ordered_ref, coeff_ref, total_ref, scratch_ref, hold_ref):
     for g in range(BAND // 8):
-        values = packed_fft([block_ref[d, 8 * g : 8 * g + 8, :] for d in range(ROWS)], -1)
-        for j in range(ROWS):
-            scratch_ref[BAND * j + 8 * g : BAND * j + 8 * g + 8, :] = NORM * values[j]
+
+        def load(d):
+            return block_ref[d, 8 * g : 8 * g + 8, :]
+
+        def store(j, value):
+            scratch_ref[BAND * j + 8 * g : BAND * j + 8 * g + 8, :] = NORM * value
+
+        across(load, store, hold_ref.at[g % 2], -1)
     total = None
     for leaf in range(LEAVES):
         x = scratch_ref[LEAF * leaf : LEAF * (leaf + 1), :]
@@ -202,7 +225,7 @@
         ),
         in_specs=[vmem] * 2,
         out_specs=(vmem,) * 3,
-        scratch_shapes=[pltpu.VMEM((LENGTH, LANES), jnp.float32)],
+        scratch_shapes=[pltpu.VMEM((LENGTH, LANES), jnp.float32), pltpu.VMEM((2, 4, 64, LANES), jnp.float32)],
         compiler_params=pltpu.CompilerParams(vmem_limit_bytes=16 * 2**20),
         cost_estimate=pl.CostEstimate(flops=10**8, bytes_accessed=2 * 2**20, transcendentals=0),
         name="coefficients",
@@ -217,7 +240,29 @@
     return [x.astype(jnp.bfloat16), times_i(x).astype(jnp.bfloat16)]
 
 
-def near_kernel(ordered_ref, coeff_ref, blocks_ref, couplings_ref, own_ref, near_ref):
+def stack_couplings(couplings_ref, first, last):
+    return jnp.concatenate(
+        [
+            jnp.concatenate(
+                [couplings_ref[leaf, t, part] for t in range(first, last) for part in range(2)], 1
+            )
+            for leaf in range(LEAVES)
+        ],
+        0,
+    )
+
+
+def near_kernel(ordered_ref, coeff_ref, blocks_ref, couplings_ref, *refs):
+    sibling_refs, own_ref, near_ref = refs[:-2], refs[-2], refs[-1]
+    known = len(sibling_refs)
+    siblings = []
+    for level in range(known):
+        siblings += with_turned(scale_of(INNER + level) * sibling_refs[level][...])
+    near_ref[...] = jnp.dot(
+        stack_couplings(couplings_ref, INNER, INNER + known),
+        jnp.concatenate(siblings, 0),
+        preferred_element_type=jnp.float32,
+    )
     for leaf in range(LEAVES):
         matrix = jnp.concatenate([blocks_ref[leaf, 0], blocks_ref[leaf, 1]], 1)
         own_ref[leaf] = jnp.dot(matrix, ordered_ref[leaf], preferred_element_type=jnp.float32)
@@ -226,46 +271,53 @@
             scale_of(1) * (coeff_ref[other] + coeff_ref[other + 1])
         )
         matrix = jnp.concatenate([couplings_ref[leaf, t, part] for t in range(INNER) for part in range(2)], 1)
-        near_ref[leaf] = jnp.dot(matrix, jnp.concatenate(siblings, 0), preferred_element_type=jnp.float32)
-
-
-def near_call(ordered, coeff, leaf_blocks, couplings):
+        near_ref[RANK * leaf : RANK * (leaf + 1), :] += jnp.dot(
+            matrix, jnp.concatenate(siblings, 0), preferred_element_type=jnp.float32
+        )
+
+
+def near_call(ordered, coeff, leaf_blocks, couplings, siblings):
     vmem = pl.BlockSpec(memory_space=pltpu.VMEM)
     return pl.pallas_call(
         near_kernel,
         out_shape=(
             jax.ShapeDtypeStruct((LEAVES, LEAF, LANES), jnp.float32),
-            jax.ShapeDtypeStruct((LEAVES, RANK, LANES), jnp.float32),
+            jax.ShapeDtypeStruct((LEAVES * RANK, LANES), jnp.float32),
         ),
-        in_specs=[vmem] * 4,
+        in_specs=[vmem] * (4 + len(siblings)),
         out_specs=(vmem,) * 2,
         compiler_params=pltpu.CompilerParams(vmem_limit_bytes=16 * 2**20),
         cost_estimate=pl.CostEstimate(flops=2 * 10**8, bytes_accessed=4 * 2**20, transcendentals=0),
         name="near_field",
-    )(ordered, coeff, leaf_blocks, couplings)
+    )(ordered, coeff, leaf_blocks, couplings, *siblings)
 
 
 def image_kernel(own_ref, near_ref, couplings_ref, basis_ref, *refs):
-    sibling_refs, out_ref, scratch_ref = refs[:UPPER], refs[UPPER], refs[UPPER + 1]
+    sibling_refs, (out_ref, scratch_ref, hold_ref) = refs[:-3], refs[-3:]
+    first = LEVELS - len(sibling_refs)
     siblings = []
-    for level in range(UPPER):
-        siblings += with_turned(scale_of(INNER + level) * sibling_refs[level][...])
-    siblings = jnp.concatenate(siblings, 0)
+    for level, ref in enumerate(sibling_refs):
+        siblings += with_turned(scale_of(first + level) * ref[...])
+    field = near_ref[...] + jnp.dot(
+        stack_couplings(couplings_ref, first, LEVELS),
+        jnp.concatenate(siblings, 0),
+        preferred_element_type=jnp.float32,
+    )
     for leaf in range(LEAVES):
-        matrix = jnp.concatenate(
-            [couplings_ref[leaf, INNER + level, part] for level in range(UPPER) for part in range(2)], 1
-        )
-        field = near_ref[leaf] + jnp.dot(matrix, siblings, preferred_element_type=jnp.float32)
         matrix = jnp.concatenate([basis_ref[leaf, 0], basis_ref[leaf, 1]], 1)
+        part = jnp.concatenate(with_turned(field[RANK * leaf : RANK * (leaf + 1)]), 0)
         scratch_ref[LEAF * leaf : LEAF * (leaf + 1), :] = own_ref[leaf] + jnp.dot(
-            matrix, jnp.concatenate(with_turned(field), 0), preferred_element_type=jnp.float32
+            matrix, part, preferred_element_type=jnp.float32
         )
     for g in range(BAND // 8):
-        values = packed_fft(
-            [scratch_ref[BAND * j + 8 * g : BAND * j + 8 * g + 8, :] for j in range(ROWS)], 1
-        )
-        for d in range(ROWS):
-            out_ref[d, 8 * g : 8 * g + 8, :] = values[d]
+
+        def load(j):
+            return scratch_ref[BAND * j + 8 * g : BAND * j + 8 * g + 8, :]
+
+        def store(d, value):
+            out_ref[d, 8 * g : 8 * g + 8, :] = value
+
+        across(load, store, hold_ref.at[g % 2], 1)
 
 
 def image_call(own, near, couplings, out_basis, siblings):
@@ -273,9 +325,9 @@
     return pl.pallas_call(
         image_kernel,
         out_shape=jax.ShapeDtypeStruct((ROWS, BAND, LANES), jnp.float32),
-        in_specs=[vmem] * (4 + UPPER),
+        in_specs=[vmem] * (4 + len(siblings)),
         out_specs=vmem,
-        scratch_shapes=[pltpu.VMEM((LENGTH, LANES), jnp.float32)],
+        scratch_shapes=[pltpu.VMEM((LENGTH, LANES), jnp.float32), pltpu.VMEM((2, 4, 64, LANES), jnp.float32)],
         compiler_params=pltpu.CompilerParams(vmem_limit_bytes=16 * 2**20),
         cost_estimate=pl.CostEstimate(flops=3 * 10**8, bytes_accessed=4 * 2**20, transcendentals=0),
         name="image",
@@ -325,13 +377,34 @@
     )(block, table)
 
 
+def partner(value, mask):
+    return lax.ppermute(value, "rows", [(i, i ^ mask) for i in range(ROWS)])
+
+
 def exchange(total):
-    held, siblings = total, []
-    for bit in range(UPPER):
-        pairs = [(i, i ^ (1 << bit)) for i in range(ROWS)]
-        siblings.append(lax.ppermute(held, "rows", pairs))
-        held = held + siblings[-1]
+    two, one, three = (partner(total, mask) for mask in (2, 1, 3))
+    held = total + one + two + three
+    siblings = [one, two + three]
+    two, one, three = (partner(held, mask) for mask in (8, 4, 12))
+    siblings += [one, two + three]
+    siblings.append(partner(held + one + two + three, 16))
     return siblings
+
+
+def second_turn():
+    token = jnp.zeros((8, HALF), jnp.float32)
+    cores = lax.axis_size("rhs")
+    for mask in (8,):
+        token = lax.ppermute(
+            token,
+            ("rows", "rhs"),
+            [
+                (cores * row + column, cores * (row ^ mask) + column)
+                for row in range(ROWS)
+                for column in range(0, cores, 2)
+            ],
+        )
+    return token
 
 
 def swap_blocks(block):
@@ -339,11 +412,11 @@
 
 
 def shards(right_side, leaf_blocks, out_basis, in_basis, couplings):
-    block = swap_blocks(forward_call(right_side))
+    block = swap_blocks(forward_call(right_side, second_turn()))
     ordered, coeff, total = coefficient_call(block, in_basis)
     siblings = exchange(total)
-    own, near = near_call(ordered, coeff, leaf_blocks, couplings)
-    return inverse_call(swap_blocks(image_call(own, near, couplings, out_basis, siblings)))
+    own, near = near_call(ordered, coeff, leaf_blocks, couplings, siblings[:EARLY])
+    return inverse_call(swap_blocks(image_call(own, near, couplings, out_basis, siblings[EARLY:])))
 
 
 def solution(mesh):

time: 110 us -> 101 us (0.918)
  starting transfers between devices: 5.69 us -> 16.1 us
  blocking collectives: 66.4 us -> 56.8 us
  waiting for transfers between devices: 29.4 us -> 20.7 us
    ppermute x5 -> x8, starting transfers between devices: 5.69 us -> 16.1 us  [the longest x7 10.9 us: partner(): return lax.ppermute(value, 'rows', [(i, i ^ mask) for i in range(ROWS)])]
    all_to_all x2, blocking collectives: 66.4 us -> 56.8 us  [swap_blocks(): lax.all_to_all(block, 'rows', split_axis=0, concat_axis=0, tiled=True)]
    ppermute x5 -> x8, waiting for transfers between devices: 29.4 us -> 20.7 us  [the longest x7 19.1 us: partner(): return lax.ppermute(value, 'rows', [(i, i ^ mask) for i in range(ROWS)])]
    pallas_call x1, Pallas kernels: 1.89 us -> 0.78 us  [image_call(): pl.pallas_call(image_kernel, out_shape=jax.ShapeDtypeStruct((ROWS, BAND,...]
  transfers between devices with their start and end apart: 5 -> 8, of which waited for: 5 -> 7; matrix products, arithmetic and copies ran while one was open for 0% -> 0% of each run, Pallas kernels for 1% -> 1%
where the time goes in v2:
time: 101 us
  blocking collectives  56.8 us (56%)
  waiting for transfers between devices  20.7 us (20%)
  starting transfers between devices  16.1 us (16%)
  Pallas kernels  5.08 us (5%)
  local copies, waits for them, and re-layouts  1.99 us (2%)
    all_to_all x2, blocking collectives, swap_blocks(): lax.all_to_all(block, 'rows', split_axis=0, concat_axis=0, tiled=True)  56.8 us
    ppermute x7, waiting for transfers between devices, partner(): return lax.ppermute(value, 'rows', [(i, i ^ mask) for i in range(ROWS)])  19.1 us
    ppermute x7, starting transfers between devices, partner(): return lax.ppermute(value, 'rows', [(i, i ^ mask) for i in range(ROWS)])  10.9 us
    ppermute x1, starting transfers between devices, second_turn(): lax.ppermute(token, ('rows', 'rhs'), [(cores * row + column, cores * (row...  5.17 us
  transfers between devices with their start and end apart: 8, of which 7 were waited for; matrix products, arithmetic and copies ran while one was open for 0% of the time, Pallas kernels for 1%

profile of v2, /device:TPU:2, one launch (start us, length us, event | category | flops | bytes accessed | tf_op | source)
XLA Modules:
  0.0 100.8 jit_solution(14056246126222750511)
XLA Ops:
  0.0 5.2 %collective-permute-start = (f32[8,128]{1,0:T(8,128)S(1)}, f32[8,128]{1,0:T(8,128)S(1)}, u32[]{:S(2)}, u32[]{:S(2)}) collective-permute-start(f32[8,128]{1,0:T(8,128)S(1)} %broadcast_in_dim.3), channel_id=1, source_target_pairs={{0,64},{2,66},{4,68},{6,70},{8,72},{10,74},{12,76},{14,78},{16,80}... | collective-permute-start | bytes 12296 | tf_op jit(solution)/shard_map/ppermute | solution.py:398
  5.2 1.6 %collective-permute-done.turn_ref = f32[8,128]{1,0:T(8,128)S(1)} collective-permute-done((f32[8,128]{1,0:T(8,128)S(1)}, f32[8,128]{1,0:T(8,128)S(1)}, u32[]{:S(2)}, u32[]{:S(2)}) %collective-permute-start) | collective-permute-done | bytes 4128 | tf_op jit(solution)/shard_map/ppermute | solution.py:398
  6.7 0.0 copy-start.3
  6.8 1.0 %copy-done.3 = f32[1024,128]{1,0:T(8,128)S(1)} copy-done((f32[1024,128]{1,0:T(8,128)S(1)}, f32[1024,128]{1,0:T(8,128)}, u32[]{:S(2)}) %copy-start.3) | copy-done | bytes 524312
  7.8 0.9 copy-done.6
  8.7 0.8 local_forward.1
  9.5 33.4 %all_to_all.10.block_ref = f32[32,32,256]{2,1,0:T(8,128)S(1)} all-to-all(f32[32,32,256]{2,1,0:T(8,128)S(1)} %local_forward.1), channel_id=1, replica_groups=mesh['rows'=32,'rhs'=8] {'rows'}, dimensions={0} | all-to-all | bytes 2097152 | tf_op jit(solution)/shard_map/all_to_all | solution.py:411
  42.9 0.0 copy-done.4
  42.9 0.7 coefficients.1
  43.7 1.5 %collective-permute-start.3 = (f32[128,256]{1,0:T(8,128)S(1)}, f32[128,256]{1,0:T(8,128)S(1)}, u32[]{:S(2)}, u32[]{:S(2)}) collective-permute-start(f32[128,256]{1,0:T(8,128)S(1)} %get-tuple-element.12), channel_id=1, source_target_pairs={{0,24},{8,16},{16,8},{24,0},{32,56},{40,48},{48,40},{56,32},{64,88... | collective-permute-start | bytes 393224 | tf_op jit(solution)/shard_map/ppermute | solution.py:381
  45.2 0.9 collective-permute-start.2
  46.1 1.7 %collective-permute-start.1 = (f32[128,256]{1,0:T(8,128)S(1)}, f32[128,256]{1,0:T(8,128)S(1)}, u32[]{:S(2)}, u32[]{:S(2)}) collective-permute-start(f32[128,256]{1,0:T(8,128)S(1)} %get-tuple-element.12), channel_id=1, source_target_pairs={{0,8},{8,0},{16,24},{24,16},{32,40},{40,32},{48,56},{56,48},{64,72... | collective-permute-start | bytes 393224 | tf_op jit(solution)/shard_map/ppermute | solution.py:381
  47.8 0.9 collective-permute-done.3
  48.7 3.0 %collective-permute-done.2 = f32[128,256]{1,0:T(8,128)S(1)} collective-permute-done((f32[128,256]{1,0:T(8,128)S(1)}, f32[128,256]{1,0:T(8,128)S(1)}, u32[]{:S(2)}, u32[]{:S(2)}) %collective-permute-start.2) | collective-permute-done | bytes 131104 | tf_op jit(solution)/shard_map/ppermute | solution.py:381
  51.7 0.5 collective-permute-done.1.refs_0_
  52.2 1.6 %collective-permute-start.6 = (f32[128,256]{1,0:T(8,128)S(1)}, f32[128,256]{1,0:T(8,128)S(1)}, u32[]{:S(2)}, u32[]{:S(2)}) collective-permute-start(f32[128,256]{1,0:T(8,128)S(1)} %get-tuple-element.17), channel_id=1, source_target_pairs={{0,96},{8,104},{16,112},{24,120},{32,64},{40,72},{48,80},{56,88},{... | collective-permute-start | bytes 393224 | tf_op jit(solution)/shard_map/ppermute | solution.py:381
  53.8 0.6 collective-permute-start.5
  54.3 2.3 %collective-permute-start.4 = (f32[128,256]{1,0:T(8,128)S(1)}, f32[128,256]{1,0:T(8,128)S(1)}, u32[]{:S(2)}, u32[]{:S(2)}) collective-permute-start(f32[128,256]{1,0:T(8,128)S(1)} %get-tuple-element.17), channel_id=1, source_target_pairs={{0,32},{8,40},{16,48},{24,56},{32,0},{40,8},{48,16},{56,24},{64,96... | collective-permute-start | bytes 393224 | tf_op jit(solution)/shard_map/ppermute | solution.py:381
  56.7 4.2 %collective-permute-done.6 = f32[128,256]{1,0:T(8,128)S(1)} collective-permute-done((f32[128,256]{1,0:T(8,128)S(1)}, f32[128,256]{1,0:T(8,128)S(1)}, u32[]{:S(2)}, u32[]{:S(2)}) %collective-permute-start.6) | collective-permute-done | bytes 131104 | tf_op jit(solution)/shard_map/ppermute | solution.py:381
  60.9 3.4 %collective-permute-done.5 = f32[128,256]{1,0:T(8,128)S(1)} collective-permute-done((f32[128,256]{1,0:T(8,128)S(1)}, f32[128,256]{1,0:T(8,128)S(1)}, u32[]{:S(2)}, u32[]{:S(2)}) %collective-permute-start.5) | collective-permute-done | bytes 131104 | tf_op jit(solution)/shard_map/ppermute | solution.py:381
  64.3 0.0 collective-permute-done.4.refs_2_
  64.4 2.2 %collective-permute-start.7 = (f32[128,256]{1,0:T(8,128)S(1)}, f32[128,256]{1,0:T(8,128)S(1)}, u32[]{:S(2)}, u32[]{:S(2)}) collective-permute-start(f32[128,256]{1,0:T(8,128)S(1)} %get-tuple-element.15), channel_id=1, source_target_pairs={{0,128},{8,136},{16,144},{24,152},{32,160},{40,168},{48,176},{56,1... | collective-permute-start | bytes 393224 | tf_op jit(solution)/shard_map/ppermute | solution.py:381
  66.6 0.0 copy-done
  66.6 0.0 copy-done.2
  66.6 0.8 near_field.1
  67.5 7.2 %collective-permute-done.7.refs_0_ = f32[128,256]{1,0:T(8,128)S(1)} collective-permute-done((f32[128,256]{1,0:T(8,128)S(1)}, f32[128,256]{1,0:T(8,128)S(1)}, u32[]{:S(2)}, u32[]{:S(2)}) %collective-permute-start.7) | collective-permute-done | bytes 131104 | tf_op jit(solution)/shard_map/ppermute | solution.py:381
  74.6 0.0 copy-done.5
  74.6 0.8 image.1
  75.4 0.0 copy-start.1
  75.4 23.4 %all_to_all.11.block_ref = f32[32,32,256]{2,1,0:T(8,128)S(1)} all-to-all(f32[32,32,256]{2,1,0:T(8,128)S(1)} %image.1), channel_id=1, replica_groups=mesh['rows'=32,'rhs'=8] {'rows'}, dimensions={0} | all-to-all | bytes 2097152 | tf_op jit(solution)/shard_map/all_to_all | solution.py:411
  98.8 0.0 copy-done.1
  98.8 2.0 %local_inverse.1 = f32[2,1024,128]{2,1,0:T(8,128)} custom-call(f32[32,32,256]{2,1,0:T(8,128)S(1)} %all_to_all.11.block_ref, bf16[8,128,768]{2,1,0:T(8,128)(2,1)S(1)} %copy-done.1), custom_call_target="tpu_custom_call" | custom-call | flops 300000000 | bytes 3145728 | tf_op jit(solution)/shard_map/local_inverse/pallas_call | solution.py:368
  (8 shorter events, 0.1 us)
Async XLA Ops:
  0.0 6.7 %collective-permute-start = (f32[8,128]{1,0:T(8,128)S(1)}, f32[8,128]{1,0:T(8,128)S(1)}, u32[]{:S(2)}, u32[]{:S(2)}) collective-permute-start(f32[8,128]{1,0:T(8,128)S(1)} %broadcast_in_dim.3), channel_id=1, source_target_pairs={{0,64},{2,66},{4,68},{6,70},{8,72},{10,74},{12,76},{14,78},{16,80}... | collective-permute-start | bytes 12296 | tf_op jit(solution)/shard_map/ppermute | solution.py:398
  6.7 1.0 %copy-start.3 = (f32[1024,128]{1,0:T(8,128)S(1)}, f32[1024,128]{1,0:T(8,128)}, u32[]{:S(2)}) copy-start(f32[1024,128]{1,0:T(8,128)} %x_ref.1) | copy-start | bytes 1572868
  7.8 0.9 copy-start.6
  8.7 34.2 %copy-start.4 = (bf16[4,2,256,128]{3,2,1,0:T(8,128)(2,1)S(1)}, bf16[4,2,256,128]{3,2,1,0:T(8,128)(2,1)}, u32[]{:S(2)}) copy-start(bf16[4,2,256,128]{3,2,1,0:T(8,128)(2,1)} %basis_ref.2) | copy-start | bytes 1572868
  42.9 23.7 %copy-start = (bf16[4,7,2,128,128]{4,3,2,1,0:T(8,128)(2,1)S(1)}, bf16[4,7,2,128,128]{4,3,2,1,0:T(8,128)(2,1)}, u32[]{:S(2)}) copy-start(bf16[4,7,2,128,128]{4,3,2,1,0:T(8,128)(2,1)} %couplings_ref.3) | copy-start | bytes 5505028
  42.9 23.7 %copy-start.2 = (bf16[4,2,256,256]{3,2,1,0:T(8,128)(2,1)S(1)}, bf16[4,2,256,256]{3,2,1,0:T(8,128)(2,1)}, u32[]{:S(2)}) copy-start(bf16[4,2,256,256]{3,2,1,0:T(8,128)(2,1)} %blocks_ref.1) | copy-start | bytes 3145732
  43.7 5.1 %collective-permute-start.3 = (f32[128,256]{1,0:T(8,128)S(1)}, f32[128,256]{1,0:T(8,128)S(1)}, u32[]{:S(2)}, u32[]{:S(2)}) collective-permute-start(f32[128,256]{1,0:T(8,128)S(1)} %get-tuple-element.12), channel_id=1, source_target_pairs={{0,24},{8,16},{16,8},{24,0},{32,56},{40,48},{48,40},{56,32},{64,88... | collective-permute-start | bytes 393224 | tf_op jit(solution)/shard_map/ppermute | solution.py:381
  45.2 6.5 %collective-permute-start.2 = (f32[128,256]{1,0:T(8,128)S(1)}, f32[128,256]{1,0:T(8,128)S(1)}, u32[]{:S(2)}, u32[]{:S(2)}) collective-permute-start(f32[128,256]{1,0:T(8,128)S(1)} %get-tuple-element.12), channel_id=1, source_target_pairs={{0,16},{8,24},{16,0},{24,8},{32,48},{40,56},{48,32},{56,40},{64,80... | collective-permute-start | bytes 393224 | tf_op jit(solution)/shard_map/ppermute | solution.py:381
  46.1 6.1 %collective-permute-start.1 = (f32[128,256]{1,0:T(8,128)S(1)}, f32[128,256]{1,0:T(8,128)S(1)}, u32[]{:S(2)}, u32[]{:S(2)}) collective-permute-start(f32[128,256]{1,0:T(8,128)S(1)} %get-tuple-element.12), channel_id=1, source_target_pairs={{0,8},{8,0},{16,24},{24,16},{32,40},{40,32},{48,56},{56,48},{64,72... | collective-permute-start | bytes 393224 | tf_op jit(solution)/shard_map/ppermute | solution.py:381
  52.2 8.7 %collective-permute-start.6 = (f32[128,256]{1,0:T(8,128)S(1)}, f32[128,256]{1,0:T(8,128)S(1)}, u32[]{:S(2)}, u32[]{:S(2)}) collective-permute-start(f32[128,256]{1,0:T(8,128)S(1)} %get-tuple-element.17), channel_id=1, source_target_pairs={{0,96},{8,104},{16,112},{24,120},{32,64},{40,72},{48,80},{56,88},{... | collective-permute-start | bytes 393224 | tf_op jit(solution)/shard_map/ppermute | solution.py:381
  53.8 10.5 %collective-permute-start.5 = (f32[128,256]{1,0:T(8,128)S(1)}, f32[128,256]{1,0:T(8,128)S(1)}, u32[]{:S(2)}, u32[]{:S(2)}) collective-permute-start(f32[128,256]{1,0:T(8,128)S(1)} %get-tuple-element.17), channel_id=1, source_target_pairs={{0,64},{8,72},{16,80},{24,88},{32,96},{40,104},{48,112},{56,120},{... | collective-permute-start | bytes 393224 | tf_op jit(solution)/shard_map/ppermute | solution.py:381
  54.3 10.0 %collective-permute-start.4 = (f32[128,256]{1,0:T(8,128)S(1)}, f32[128,256]{1,0:T(8,128)S(1)}, u32[]{:S(2)}, u32[]{:S(2)}) collective-permute-start(f32[128,256]{1,0:T(8,128)S(1)} %get-tuple-element.17), channel_id=1, source_target_pairs={{0,32},{8,40},{16,48},{24,56},{32,0},{40,8},{48,16},{56,24},{64,96... | collective-permute-start | bytes 393224 | tf_op jit(solution)/shard_map/ppermute | solution.py:381
  64.4 10.3 %collective-permute-start.7 = (f32[128,256]{1,0:T(8,128)S(1)}, f32[128,256]{1,0:T(8,128)S(1)}, u32[]{:S(2)}, u32[]{:S(2)}) collective-permute-start(f32[128,256]{1,0:T(8,128)S(1)} %get-tuple-element.15), channel_id=1, source_target_pairs={{0,128},{8,136},{16,144},{24,152},{32,160},{40,168},{48,176},{56,1... | collective-permute-start | bytes 393224 | tf_op jit(solution)/shard_map/ppermute | solution.py:381
  66.6 8.0 %copy-start.5 = (bf16[4,2,256,128]{3,2,1,0:T(8,128)(2,1)S(1)}, bf16[4,2,256,128]{3,2,1,0:T(8,128)(2,1)}, u32[]{:S(2)}) copy-start(bf16[4,2,256,128]{3,2,1,0:T(8,128)(2,1)} %basis_ref.3) | copy-start | bytes 1572868
  75.4 23.4 %copy-start.1 = (bf16[8,128,768]{2,1,0:T(8,128)(2,1)S(1)}, bf16[8,128,768]{2,1,0:T(8,128)(2,1)}, u32[]{:S(2)}) copy-start(bf16[8,128,768]{2,1,0:T(8,128)(2,1)} %constant.7.clone.table_ref) | copy-start | bytes 4718596

commit v3 on v2

--- a/solution.py
+++ b/solution.py
@@ -31,14 +31,6 @@
     high = table.astype(ml_dtypes.bfloat16)
     low = (table - high.astype(np.float64)).astype(ml_dtypes.bfloat16)
     return high, low
-
-
-def forward_table():
-    k = np.arange(POINTS)[:, None]
-    a = np.arange(POINTS)[None, :]
-    angle = -2.0 * np.pi * ((a * k) % POINTS) / POINTS
-    high, low = split_table(np.concatenate([np.cos(angle), np.sin(angle)], 0))
-    return np.concatenate([high, low, high], 1)
 
 
 def inverse_tables():
@@ -144,9 +136,23 @@
     return small_phase(row * (device * scale if isinstance(device, int) else device.astype(jnp.float32) * scale))
 
 
-def forward_kernel(x_ref, table_ref, turn_ref, out_ref, part_ref):
+def forward_table():
+    k = lax.broadcasted_iota(jnp.int32, (POINTS, POINTS), 0)
+    a = lax.broadcasted_iota(jnp.int32, (POINTS, POINTS), 1)
+    turns = jnp.bitwise_and(k * a, POINTS - 1)
+    turns = jnp.where(turns < POINTS // 2, turns, turns - POINTS).astype(jnp.float32)
+    phase = small_phase(turns * (-2.0 * math.pi / (4 * POINTS)))
+    for _ in range(2):
+        phase = cmul(phase, phase)
+    table = jnp.concatenate(phase, 0)
+    high = table.astype(jnp.bfloat16)
+    low = (table - high.astype(jnp.float32)).astype(jnp.bfloat16)
+    return jnp.concatenate([high, low, high], 1)
+
+
+def forward_kernel(x_ref, turn_ref, out_ref, part_ref):
     device = lax.axis_index("rows")
-    table = table_ref[...]
+    table = forward_table()
     for pair in range(RADIX // 2):
         x = jnp.concatenate([x_ref[pl.ds(2 * pair + i, POINTS, stride=RADIX), :] for i in range(2)], 1)
         high = x.astype(jnp.bfloat16)
@@ -173,18 +179,17 @@
 
 def forward_call(x, turn):
     shape = jax.ShapeDtypeStruct((ROWS, BAND, LANES), jnp.float32)
-    table = jnp.asarray(forward_table())
     vmem = pl.BlockSpec(memory_space=pltpu.VMEM)
     return pl.pallas_call(
         forward_kernel,
         out_shape=shape,
-        in_specs=[vmem, vmem, pl.BlockSpec(memory_space=pl.ANY)],
+        in_specs=[vmem, pl.BlockSpec(memory_space=pl.ANY)],
         out_specs=vmem,
         scratch_shapes=[pltpu.VMEM((RADIX, 2 * POINTS, HALF), jnp.float32)],
         compiler_params=pltpu.CompilerParams(vmem_limit_bytes=16 * 2**20),
         cost_estimate=pl.CostEstimate(flops=3 * 10**8, bytes_accessed=3 * 2**20, transcendentals=0),
         name="local_forward",
-    )(x, table, turn)
+    )(x, turn)
 
 
 def transposed_dot(left, right):

time: 101 us -> 100 us (0.990)
  no operation moved by 1% of the time
where the time goes in v3:
time: 100 us; the launch traced here: 99.9 us
  blocking collectives  56.8 us (57%)
  waiting for transfers between devices  20.7 us (21%)
  starting transfers between devices  16.1 us (16%)
  Pallas kernels  5.16 us (5%)
  local copies, waits for them, and re-layouts  1.06 us (1%)
    all_to_all x2, blocking collectives, swap_blocks(): lax.all_to_all(block, 'rows', split_axis=0, concat_axis=0, tiled=True)  56.8 us
    ppermute x7, waiting for transfers between devices, partner(): return lax.ppermute(value, 'rows', [(i, i ^ mask) for i in range(ROWS)])  19.1 us
    ppermute x7, starting transfers between devices, partner(): return lax.ppermute(value, 'rows', [(i, i ^ mask) for i in range(ROWS)])  10.9 us
    ppermute x1, starting transfers between devices, second_turn(): lax.ppermute(token, ('rows', 'rhs'), [(cores * row + column, cores * (row...  5.17 us
  transfers between devices with their start and end apart: 8, of which 7 were waited for; matrix products, arithmetic and copies ran while one was open for 0% of the time, Pallas kernels for 1%

profile of v3, /device:TPU:2, one launch (start us, length us, event | category | flops | bytes accessed | tf_op | source)
XLA Modules:
  0.0 99.9 jit_solution(18317236275329024933)
XLA Ops:
  0.0 5.2 %collective-permute-start = (f32[8,128]{1,0:T(8,128)S(1)}, f32[8,128]{1,0:T(8,128)S(1)}, u32[]{:S(2)}, u32[]{:S(2)}) collective-permute-start(f32[8,128]{1,0:T(8,128)S(1)} %broadcast_in_dim.3), channel_id=1, source_target_pairs={{0,64},{2,66},{4,68},{6,70},{8,72},{10,74},{12,76},{14,78},{16,80}... | collective-permute-start | bytes 12296 | tf_op jit(solution)/shard_map/ppermute | solution.py:403
  5.2 1.6 %collective-permute-done.turn_ref = f32[8,128]{1,0:T(8,128)S(1)} collective-permute-done((f32[8,128]{1,0:T(8,128)S(1)}, f32[8,128]{1,0:T(8,128)S(1)}, u32[]{:S(2)}, u32[]{:S(2)}) %collective-permute-start) | collective-permute-done | bytes 4128 | tf_op jit(solution)/shard_map/ppermute | solution.py:403
  6.8 1.0 %copy-done.3 = f32[1024,128]{1,0:T(8,128)S(1)} copy-done((f32[1024,128]{1,0:T(8,128)S(1)}, f32[1024,128]{1,0:T(8,128)}, u32[]{:S(2)}) %copy-start.3) | copy-done | bytes 524312
  7.8 0.0 copy-start.4
  7.8 0.9 local_forward.1
  8.7 33.4 %all_to_all.10.block_ref = f32[32,32,256]{2,1,0:T(8,128)S(1)} all-to-all(f32[32,32,256]{2,1,0:T(8,128)S(1)} %local_forward.1), channel_id=1, replica_groups=mesh['rows'=32,'rhs'=8] {'rows'}, dimensions={0} | all-to-all | bytes 2097152 | tf_op jit(solution)/shard_map/all_to_all | solution.py:416
  42.1 0.0 copy-done.4
  42.1 0.0 copy-start
  42.1 0.7 coefficients.1
  42.8 1.6 %collective-permute-start.3 = (f32[128,256]{1,0:T(8,128)S(1)}, f32[128,256]{1,0:T(8,128)S(1)}, u32[]{:S(2)}, u32[]{:S(2)}) collective-permute-start(f32[128,256]{1,0:T(8,128)S(1)} %get-tuple-element.12), channel_id=1, source_target_pairs={{0,24},{8,16},{16,8},{24,0},{32,56},{40,48},{48,40},{56,32},{64,88... | collective-permute-start | bytes 393224 | tf_op jit(solution)/shard_map/ppermute | solution.py:386
  44.3 0.9 collective-permute-start.2
  45.3 1.7 %collective-permute-start.1 = (f32[128,256]{1,0:T(8,128)S(1)}, f32[128,256]{1,0:T(8,128)S(1)}, u32[]{:S(2)}, u32[]{:S(2)}) collective-permute-start(f32[128,256]{1,0:T(8,128)S(1)} %get-tuple-element.12), channel_id=1, source_target_pairs={{0,8},{8,0},{16,24},{24,16},{32,40},{40,32},{48,56},{56,48},{64,72... | collective-permute-start | bytes 393224 | tf_op jit(solution)/shard_map/ppermute | solution.py:386
  47.0 0.9 collective-permute-done.3
  47.9 3.0 %collective-permute-done.2 = f32[128,256]{1,0:T(8,128)S(1)} collective-permute-done((f32[128,256]{1,0:T(8,128)S(1)}, f32[128,256]{1,0:T(8,128)S(1)}, u32[]{:S(2)}, u32[]{:S(2)}) %collective-permute-start.2) | collective-permute-done | bytes 131104 | tf_op jit(solution)/shard_map/ppermute | solution.py:386
  50.8 0.5 collective-permute-done.1.refs_0_
  51.4 1.6 %collective-permute-start.6 = (f32[128,256]{1,0:T(8,128)S(1)}, f32[128,256]{1,0:T(8,128)S(1)}, u32[]{:S(2)}, u32[]{:S(2)}) collective-permute-start(f32[128,256]{1,0:T(8,128)S(1)} %get-tuple-element.17), channel_id=1, source_target_pairs={{0,96},{8,104},{16,112},{24,120},{32,64},{40,72},{48,80},{56,88},{... | collective-permute-start | bytes 393224 | tf_op jit(solution)/shard_map/ppermute | solution.py:386
  52.9 0.6 collective-permute-start.5
  53.5 2.3 %collective-permute-start.4 = (f32[128,256]{1,0:T(8,128)S(1)}, f32[128,256]{1,0:T(8,128)S(1)}, u32[]{:S(2)}, u32[]{:S(2)}) collective-permute-start(f32[128,256]{1,0:T(8,128)S(1)} %get-tuple-element.17), channel_id=1, source_target_pairs={{0,32},{8,40},{16,48},{24,56},{32,0},{40,8},{48,16},{56,24},{64,96... | collective-permute-start | bytes 393224 | tf_op jit(solution)/shard_map/ppermute | solution.py:386
  55.8 4.2 %collective-permute-done.6 = f32[128,256]{1,0:T(8,128)S(1)} collective-permute-done((f32[128,256]{1,0:T(8,128)S(1)}, f32[128,256]{1,0:T(8,128)S(1)}, u32[]{:S(2)}, u32[]{:S(2)}) %collective-permute-start.6) | collective-permute-done | bytes 131104 | tf_op jit(solution)/shard_map/ppermute | solution.py:386
  60.1 3.4 %collective-permute-done.5 = f32[128,256]{1,0:T(8,128)S(1)} collective-permute-done((f32[128,256]{1,0:T(8,128)S(1)}, f32[128,256]{1,0:T(8,128)S(1)}, u32[]{:S(2)}, u32[]{:S(2)}) %collective-permute-start.5) | collective-permute-done | bytes 131104 | tf_op jit(solution)/shard_map/ppermute | solution.py:386
  63.5 0.0 collective-permute-done.4.refs_2_
  63.5 2.2 %collective-permute-start.7 = (f32[128,256]{1,0:T(8,128)S(1)}, f32[128,256]{1,0:T(8,128)S(1)}, u32[]{:S(2)}, u32[]{:S(2)}) collective-permute-start(f32[128,256]{1,0:T(8,128)S(1)} %get-tuple-element.15), channel_id=1, source_target_pairs={{0,128},{8,136},{16,144},{24,152},{32,160},{40,168},{48,176},{56,1... | collective-permute-start | bytes 393224 | tf_op jit(solution)/shard_map/ppermute | solution.py:386
  65.7 0.0 copy-done
  65.7 0.0 copy-done.2
  65.7 0.8 near_field.1
  66.6 7.2 %collective-permute-done.7.refs_0_ = f32[128,256]{1,0:T(8,128)S(1)} collective-permute-done((f32[128,256]{1,0:T(8,128)S(1)}, f32[128,256]{1,0:T(8,128)S(1)}, u32[]{:S(2)}, u32[]{:S(2)}) %collective-permute-start.7) | collective-permute-done | bytes 131104 | tf_op jit(solution)/shard_map/ppermute | solution.py:386
  73.8 0.0 copy-done.5
  73.8 0.8 image.1
  74.6 0.0 copy-start.1
  74.6 23.4 %all_to_all.11.block_ref = f32[32,32,256]{2,1,0:T(8,128)S(1)} all-to-all(f32[32,32,256]{2,1,0:T(8,128)S(1)} %image.1), channel_id=1, replica_groups=mesh['rows'=32,'rhs'=8] {'rows'}, dimensions={0} | all-to-all | bytes 2097152 | tf_op jit(solution)/shard_map/all_to_all | solution.py:416
  97.9 0.0 copy-done.1
  98.0 2.0 %local_inverse.1 = f32[2,1024,128]{2,1,0:T(8,128)} custom-call(f32[32,32,256]{2,1,0:T(8,128)S(1)} %all_to_all.11.block_ref, bf16[8,128,768]{2,1,0:T(8,128)(2,1)S(1)} %copy-done.1), custom_call_target="tpu_custom_call" | custom-call | flops 300000000 | bytes 3145728 | tf_op jit(solution)/shard_map/local_inverse/pallas_call | solution.py:373
  (6 shorter events, 0.1 us)
Async XLA Ops:
  0.0 6.7 %collective-permute-start = (f32[8,128]{1,0:T(8,128)S(1)}, f32[8,128]{1,0:T(8,128)S(1)}, u32[]{:S(2)}, u32[]{:S(2)}) collective-permute-start(f32[8,128]{1,0:T(8,128)S(1)} %broadcast_in_dim.3), channel_id=1, source_target_pairs={{0,64},{2,66},{4,68},{6,70},{8,72},{10,74},{12,76},{14,78},{16,80}... | collective-permute-start | bytes 12296 | tf_op jit(solution)/shard_map/ppermute | solution.py:403
  6.7 1.0 %copy-start.3 = (f32[1024,128]{1,0:T(8,128)S(1)}, f32[1024,128]{1,0:T(8,128)}, u32[]{:S(2)}) copy-start(f32[1024,128]{1,0:T(8,128)} %x_ref.1) | copy-start | bytes 1572868
  7.8 34.3 %copy-start.4 = (bf16[4,2,256,128]{3,2,1,0:T(8,128)(2,1)S(1)}, bf16[4,2,256,128]{3,2,1,0:T(8,128)(2,1)}, u32[]{:S(2)}) copy-start(bf16[4,2,256,128]{3,2,1,0:T(8,128)(2,1)} %basis_ref.2) | copy-start | bytes 1572868
  42.1 23.7 %copy-start = (bf16[4,7,2,128,128]{4,3,2,1,0:T(8,128)(2,1)S(1)}, bf16[4,7,2,128,128]{4,3,2,1,0:T(8,128)(2,1)}, u32[]{:S(2)}) copy-start(bf16[4,7,2,128,128]{4,3,2,1,0:T(8,128)(2,1)} %couplings_ref.3) | copy-start | bytes 5505028
  42.1 23.7 %copy-start.2 = (bf16[4,2,256,256]{3,2,1,0:T(8,128)(2,1)S(1)}, bf16[4,2,256,256]{3,2,1,0:T(8,128)(2,1)}, u32[]{:S(2)}) copy-start(bf16[4,2,256,256]{3,2,1,0:T(8,128)(2,1)} %blocks_ref.1) | copy-start | bytes 3145732
  42.8 5.1 %collective-permute-start.3 = (f32[128,256]{1,0:T(8,128)S(1)}, f32[128,256]{1,0:T(8,128)S(1)}, u32[]{:S(2)}, u32[]{:S(2)}) collective-permute-start(f32[128,256]{1,0:T(8,128)S(1)} %get-tuple-element.12), channel_id=1, source_target_pairs={{0,24},{8,16},{16,8},{24,0},{32,56},{40,48},{48,40},{56,32},{64,88... | collective-permute-start | bytes 393224 | tf_op jit(solution)/shard_map/ppermute | solution.py:386
  44.3 6.5 %collective-permute-start.2 = (f32[128,256]{1,0:T(8,128)S(1)}, f32[128,256]{1,0:T(8,128)S(1)}, u32[]{:S(2)}, u32[]{:S(2)}) collective-permute-start(f32[128,256]{1,0:T(8,128)S(1)} %get-tuple-element.12), channel_id=1, source_target_pairs={{0,16},{8,24},{16,0},{24,8},{32,48},{40,56},{48,32},{56,40},{64,80... | collective-permute-start | bytes 393224 | tf_op jit(solution)/shard_map/ppermute | solution.py:386
  45.3 6.1 %collective-permute-start.1 = (f32[128,256]{1,0:T(8,128)S(1)}, f32[128,256]{1,0:T(8,128)S(1)}, u32[]{:S(2)}, u32[]{:S(2)}) collective-permute-start(f32[128,256]{1,0:T(8,128)S(1)} %get-tuple-element.12), channel_id=1, source_target_pairs={{0,8},{8,0},{16,24},{24,16},{32,40},{40,32},{48,56},{56,48},{64,72... | collective-permute-start | bytes 393224 | tf_op jit(solution)/shard_map/ppermute | solution.py:386
  51.4 8.7 %collective-permute-start.6 = (f32[128,256]{1,0:T(8,128)S(1)}, f32[128,256]{1,0:T(8,128)S(1)}, u32[]{:S(2)}, u32[]{:S(2)}) collective-permute-start(f32[128,256]{1,0:T(8,128)S(1)} %get-tuple-element.17), channel_id=1, source_target_pairs={{0,96},{8,104},{16,112},{24,120},{32,64},{40,72},{48,80},{56,88},{... | collective-permute-start | bytes 393224 | tf_op jit(solution)/shard_map/ppermute | solution.py:386
  52.9 10.5 %collective-permute-start.5 = (f32[128,256]{1,0:T(8,128)S(1)}, f32[128,256]{1,0:T(8,128)S(1)}, u32[]{:S(2)}, u32[]{:S(2)}) collective-permute-start(f32[128,256]{1,0:T(8,128)S(1)} %get-tuple-element.17), channel_id=1, source_target_pairs={{0,64},{8,72},{16,80},{24,88},{32,96},{40,104},{48,112},{56,120},{... | collective-permute-start | bytes 393224 | tf_op jit(solution)/shard_map/ppermute | solution.py:386
  53.5 10.0 %collective-permute-start.4 = (f32[128,256]{1,0:T(8,128)S(1)}, f32[128,256]{1,0:T(8,128)S(1)}, u32[]{:S(2)}, u32[]{:S(2)}) collective-permute-start(f32[128,256]{1,0:T(8,128)S(1)} %get-tuple-element.17), channel_id=1, source_target_pairs={{0,32},{8,40},{16,48},{24,56},{32,0},{40,8},{48,16},{56,24},{64,96... | collective-permute-start | bytes 393224 | tf_op jit(solution)/shard_map/ppermute | solution.py:386
  63.5 10.3 %collective-permute-start.7 = (f32[128,256]{1,0:T(8,128)S(1)}, f32[128,256]{1,0:T(8,128)S(1)}, u32[]{:S(2)}, u32[]{:S(2)}) collective-permute-start(f32[128,256]{1,0:T(8,128)S(1)} %get-tuple-element.15), channel_id=1, source_target_pairs={{0,128},{8,136},{16,144},{24,152},{32,160},{40,168},{48,176},{56,1... | collective-permute-start | bytes 393224 | tf_op jit(solution)/shard_map/ppermute | solution.py:386
  65.7 8.0 %copy-start.5 = (bf16[4,2,256,128]{3,2,1,0:T(8,128)(2,1)S(1)}, bf16[4,2,256,128]{3,2,1,0:T(8,128)(2,1)}, u32[]{:S(2)}) copy-start(bf16[4,2,256,128]{3,2,1,0:T(8,128)(2,1)} %basis_ref.3) | copy-start | bytes 1572868
  74.6 23.4 %copy-start.1 = (bf16[8,128,768]{2,1,0:T(8,128)(2,1)S(1)}, bf16[8,128,768]{2,1,0:T(8,128)(2,1)}, u32[]{:S(2)}) copy-start(bf16[8,128,768]{2,1,0:T(8,128)(2,1)} %constant.4.clone.table_ref) | copy-start | bytes 4718596

commit v4 on v3

--- a/solution.py
+++ b/solution.py
@@ -22,6 +22,7 @@
 LEAVES = 4
 INNER = 2
 UPPER = 5
+PIECES = 2
 EARLY = 4
 RADIX = 8
 POINTS = LENGTH // RADIX
@@ -38,8 +39,9 @@
     a = np.arange(POINTS)[None, :, None]
     k = np.arange(POINTS)[None, None, :]
     angle = 2.0 * np.pi * (((8 * a + b) * k) % LENGTH) / LENGTH
-    high, low = split_table(NORM * np.concatenate([np.cos(angle), np.sin(angle)], 2))
-    return np.concatenate([high, low, high], 2)
+    parts = split_table(NORM * np.concatenate([np.cos(angle), np.sin(angle)], 2))
+    parts = [part.reshape(RADIX, PIECES, POINTS // PIECES, 2 * POINTS) for part in parts]
+    return np.concatenate(parts, 2)
 
 
 def times_i(x):
@@ -339,32 +341,50 @@
     )(own, near, couplings, out_basis, *siblings)
 
 
-def inverse_kernel(block_ref, table_ref, out_ref, turned_ref):
+def inverse_kernel(block_ref, table_ref, out_ref, turned_ref, stage_ref, sems):
     device = lax.axis_index("rows")
     blocks = block_phases(device, 1.0)
-    for g in range(POINTS // 8):
-        rows = row_phase(device, 8 * g, 1.0)
-        values = []
-        for k in range(RADIX):
-            phase = rows if k == 0 else cmul(rows, blocks[k])
-            at = POINTS * k + 8 * g
-            x = block_ref[at // BAND, at % BAND : at % BAND + 8, :]
-            values.append(jnp.concatenate(cmul((x[:, :HALF], x[:, HALF:]), phase), 1))
-        values = packed_fft(values, 1)
+    for g in range(POINTS // 16):
+        halves = []
+        for start in (16 * g, 16 * g + 8):
+            rows = row_phase(device, start, 1.0)
+            values = []
+            for k in range(RADIX):
+                phase = rows if k == 0 else cmul(rows, blocks[k])
+                at = POINTS * k + start
+                x = block_ref[at // BAND, at % BAND : at % BAND + 8, :]
+                values.append(cmul((x[:, :HALF], x[:, HALF:]), phase))
+            halves.append(split_fft(values, 1))
         for b in range(RADIX):
-            turned_ref[b, 8 * g : 8 * g + 8, :] = values[b]
-    for b in range(RADIX):
-        x = turned_ref[b]
-        high = x.astype(jnp.bfloat16)
-        low = (x - high.astype(jnp.float32)).astype(jnp.bfloat16)
-        high_y, low_y = times_i(high), times_i(low)
-        value = jnp.dot(
-            table_ref[b],
-            jnp.concatenate([high, high_y, high, high_y, low, low_y], 0),
-            preferred_element_type=jnp.float32,
-        )
-        out_ref[0, pl.ds(b, POINTS, stride=RADIX), :] = value[:, :HALF]
-        out_ref[1, pl.ds(b, POINTS, stride=RADIX), :] = value[:, HALF:]
+            re, im = (jnp.concatenate([half[b][part] for half in halves], 0) for part in range(2))
+            rows = slice(16 * g, 16 * g + 16)
+            turned_ref[b, rows, :HALF] = re.astype(jnp.bfloat16)
+            turned_ref[b, rows, HALF:] = im.astype(jnp.bfloat16)
+            rows = slice(POINTS + 16 * g, POINTS + 16 * g + 16)
+            turned_ref[b, rows, :HALF] = (-im).astype(jnp.bfloat16)
+            turned_ref[b, rows, HALF:] = re.astype(jnp.bfloat16)
+    count = POINTS // PIECES
+    copies = []
+    for piece in range(PIECES):
+        for b in range(RADIX):
+            value = jnp.dot(table_ref[b, piece], turned_ref[b], preferred_element_type=jnp.float32)
+            value = value[:count] + value[count:]
+            for part in range(2):
+                rows = pl.ds(RADIX * count * piece + b, count, stride=RADIX)
+                stage_ref[part, rows, :] = value[:, HALF * part : HALF * (part + 1)]
+        for part in range(2):
+            for half in range(2):
+                rows = pl.ds(RADIX * count * piece + RADIX * count // 2 * half, RADIX * count // 2)
+                copies.append(
+                    pltpu.make_async_copy(
+                        stage_ref.at[part, rows, :],
+                        out_ref.at[part, rows, :],
+                        sems.at[4 * piece + 2 * part + half],
+                    )
+                )
+                copies[-1].start()
+    for copy in copies:
+        copy.wait()
 
 
 def inverse_call(block):
@@ -374,8 +394,12 @@
         inverse_kernel,
         out_shape=jax.ShapeDtypeStruct((2, LENGTH, HALF), jnp.float32),
         in_specs=[vmem] * 2,
-        out_specs=vmem,
-        scratch_shapes=[pltpu.VMEM((RADIX, POINTS, LANES), jnp.float32)],
+        out_specs=pl.BlockSpec(memory_space=pltpu.HBM),
+        scratch_shapes=[
+            pltpu.VMEM((RADIX, 2 * POINTS, LANES), jnp.bfloat16),
+            pltpu.VMEM((2, LENGTH, HALF), jnp.float32),
+            pltpu.SemaphoreType.DMA((4 * PIECES,)),
+        ],
         compiler_params=pltpu.CompilerParams(vmem_limit_bytes=16 * 2**20),
         cost_estimate=pl.CostEstimate(flops=3 * 10**8, bytes_accessed=3 * 2**20, transcendentals=0),
         name="local_inverse",

time: 100 us -> 100 us (level)
  no operation moved by 1% of the time
where the time goes in v4:
time: 100 us; the launch traced here: 99.7 us
  blocking collectives  56.8 us (57%)
  waiting for transfers between devices  20.7 us (21%)
  starting transfers between devices  16.1 us (16%)
  Pallas kernels  4.96 us (5%)
  local copies, waits for them, and re-layouts  1.06 us (1%)
    all_to_all x2, blocking collectives, swap_blocks(): lax.all_to_all(block, 'rows', split_axis=0, concat_axis=0, tiled=True)  56.8 us
    ppermute x7, waiting for transfers between devices, partner(): return lax.ppermute(value, 'rows', [(i, i ^ mask) for i in range(ROWS)])  19.1 us
    ppermute x7, starting transfers between devices, partner(): return lax.ppermute(value, 'rows', [(i, i ^ mask) for i in range(ROWS)])  10.9 us
    ppermute x1, starting transfers between devices, second_turn(): lax.ppermute(token, ('rows', 'rhs'), [(cores * row + column, cores * (row...  5.17 us
  transfers between devices with their start and end apart: 8, of which 7 were waited for; matrix products, arithmetic and copies ran while one was open for 0% of the time, Pallas kernels for 1%

profile of v4, /device:TPU:2, one launch (start us, length us, event | category | flops | bytes accessed | tf_op | source)
XLA Modules:
  0.0 99.7 jit_solution(7196914327781415832)
XLA Ops:
  0.0 5.2 %collective-permute-start = (f32[8,128]{1,0:T(8,128)S(1)}, f32[8,128]{1,0:T(8,128)S(1)}, u32[]{:S(2)}, u32[]{:S(2)}) collective-permute-start(f32[8,128]{1,0:T(8,128)S(1)} %broadcast_in_dim.3), channel_id=1, source_target_pairs={{0,64},{2,66},{4,68},{6,70},{8,72},{10,74},{12,76},{14,78},{16,80}... | collective-permute-start | bytes 12296 | tf_op jit(solution)/shard_map/ppermute | solution.py:427
  5.2 1.6 %collective-permute-done.turn_ref = f32[8,128]{1,0:T(8,128)S(1)} collective-permute-done((f32[8,128]{1,0:T(8,128)S(1)}, f32[8,128]{1,0:T(8,128)S(1)}, u32[]{:S(2)}, u32[]{:S(2)}) %collective-permute-start) | collective-permute-done | bytes 4128 | tf_op jit(solution)/shard_map/ppermute | solution.py:427
  6.7 0.0 copy-start.3
  6.8 1.0 %copy-done.3 = f32[1024,128]{1,0:T(8,128)S(1)} copy-done((f32[1024,128]{1,0:T(8,128)S(1)}, f32[1024,128]{1,0:T(8,128)}, u32[]{:S(2)}) %copy-start.3) | copy-done | bytes 524312
  7.8 0.0 copy-start.4
  7.8 0.9 local_forward.1
  8.7 33.4 %all_to_all.10.block_ref = f32[32,32,256]{2,1,0:T(8,128)S(1)} all-to-all(f32[32,32,256]{2,1,0:T(8,128)S(1)} %local_forward.1), channel_id=1, replica_groups=mesh['rows'=32,'rhs'=8] {'rows'}, dimensions={0} | all-to-all | bytes 2097152 | tf_op jit(solution)/shard_map/all_to_all | solution.py:440
  42.1 0.0 copy-done.4
  42.1 0.7 coefficients.1
  42.8 1.6 %collective-permute-start.3 = (f32[128,256]{1,0:T(8,128)S(1)}, f32[128,256]{1,0:T(8,128)S(1)}, u32[]{:S(2)}, u32[]{:S(2)}) collective-permute-start(f32[128,256]{1,0:T(8,128)S(1)} %get-tuple-element.12), channel_id=1, source_target_pairs={{0,24},{8,16},{16,8},{24,0},{32,56},{40,48},{48,40},{56,32},{64,88... | collective-permute-start | bytes 393224 | tf_op jit(solution)/shard_map/ppermute | solution.py:410
  44.3 0.9 collective-permute-start.2
  45.3 1.7 %collective-permute-start.1 = (f32[128,256]{1,0:T(8,128)S(1)}, f32[128,256]{1,0:T(8,128)S(1)}, u32[]{:S(2)}, u32[]{:S(2)}) collective-permute-start(f32[128,256]{1,0:T(8,128)S(1)} %get-tuple-element.12), channel_id=1, source_target_pairs={{0,8},{8,0},{16,24},{24,16},{32,40},{40,32},{48,56},{56,48},{64,72... | collective-permute-start | bytes 393224 | tf_op jit(solution)/shard_map/ppermute | solution.py:410
  47.0 0.9 collective-permute-done.3
  47.9 3.0 %collective-permute-done.2 = f32[128,256]{1,0:T(8,128)S(1)} collective-permute-done((f32[128,256]{1,0:T(8,128)S(1)}, f32[128,256]{1,0:T(8,128)S(1)}, u32[]{:S(2)}, u32[]{:S(2)}) %collective-permute-start.2) | collective-permute-done | bytes 131104 | tf_op jit(solution)/shard_map/ppermute | solution.py:410
  50.8 0.5 collective-permute-done.1.refs_0_
  51.4 1.6 %collective-permute-start.6 = (f32[128,256]{1,0:T(8,128)S(1)}, f32[128,256]{1,0:T(8,128)S(1)}, u32[]{:S(2)}, u32[]{:S(2)}) collective-permute-start(f32[128,256]{1,0:T(8,128)S(1)} %get-tuple-element.17), channel_id=1, source_target_pairs={{0,96},{8,104},{16,112},{24,120},{32,64},{40,72},{48,80},{56,88},{... | collective-permute-start | bytes 393224 | tf_op jit(solution)/shard_map/ppermute | solution.py:410
  52.9 0.6 collective-permute-start.5
  53.5 2.3 %collective-permute-start.4 = (f32[128,256]{1,0:T(8,128)S(1)}, f32[128,256]{1,0:T(8,128)S(1)}, u32[]{:S(2)}, u32[]{:S(2)}) collective-permute-start(f32[128,256]{1,0:T(8,128)S(1)} %get-tuple-element.17), channel_id=1, source_target_pairs={{0,32},{8,40},{16,48},{24,56},{32,0},{40,8},{48,16},{56,24},{64,96... | collective-permute-start | bytes 393224 | tf_op jit(solution)/shard_map/ppermute | solution.py:410
  55.8 4.2 %collective-permute-done.6 = f32[128,256]{1,0:T(8,128)S(1)} collective-permute-done((f32[128,256]{1,0:T(8,128)S(1)}, f32[128,256]{1,0:T(8,128)S(1)}, u32[]{:S(2)}, u32[]{:S(2)}) %collective-permute-start.6) | collective-permute-done | bytes 131104 | tf_op jit(solution)/shard_map/ppermute | solution.py:410
  60.1 3.4 %collective-permute-done.5 = f32[128,256]{1,0:T(8,128)S(1)} collective-permute-done((f32[128,256]{1,0:T(8,128)S(1)}, f32[128,256]{1,0:T(8,128)S(1)}, u32[]{:S(2)}, u32[]{:S(2)}) %collective-permute-start.5) | collective-permute-done | bytes 131104 | tf_op jit(solution)/shard_map/ppermute | solution.py:410
  63.5 0.0 collective-permute-done.4.refs_2_
  63.5 2.2 %collective-permute-start.7 = (f32[128,256]{1,0:T(8,128)S(1)}, f32[128,256]{1,0:T(8,128)S(1)}, u32[]{:S(2)}, u32[]{:S(2)}) collective-permute-start(f32[128,256]{1,0:T(8,128)S(1)} %get-tuple-element.15), channel_id=1, source_target_pairs={{0,128},{8,136},{16,144},{24,152},{32,160},{40,168},{48,176},{56,1... | collective-permute-start | bytes 393224 | tf_op jit(solution)/shard_map/ppermute | solution.py:410
  65.7 0.0 copy-done
  65.7 0.0 copy-done.1
  65.7 0.8 near_field.1
  66.6 7.2 %collective-permute-done.7.refs_0_ = f32[128,256]{1,0:T(8,128)S(1)} collective-permute-done((f32[128,256]{1,0:T(8,128)S(1)}, f32[128,256]{1,0:T(8,128)S(1)}, u32[]{:S(2)}, u32[]{:S(2)}) %collective-permute-start.7) | collective-permute-done | bytes 131104 | tf_op jit(solution)/shard_map/ppermute | solution.py:410
  73.8 0.0 copy-done.5
  73.8 0.8 image.1
  74.6 0.0 copy-start.2
  74.6 23.4 %all_to_all.11.block_ref = f32[32,32,256]{2,1,0:T(8,128)S(1)} all-to-all(f32[32,32,256]{2,1,0:T(8,128)S(1)} %image.1), channel_id=1, replica_groups=mesh['rows'=32,'rhs'=8] {'rows'}, dimensions={0} | all-to-all | bytes 2097152 | tf_op jit(solution)/shard_map/all_to_all | solution.py:440
  97.9 0.0 copy-done.2
  98.0 1.7 %local_inverse.1 = f32[2,1024,128]{2,1,0:T(8,128)} custom-call(f32[32,32,256]{2,1,0:T(8,128)S(1)} %all_to_all.11.block_ref, bf16[8,2,128,256]{3,2,1,0:T(8,128)(2,1)S(1)} %copy-done.2), custom_call_target="tpu_custom_call" | custom-call | flops 300000000 | bytes 3145728 | tf_op jit(solution)/shard_map/local_inverse/pallas_call | solution.py:393
  (6 shorter events, 0.1 us)
Async XLA Ops:
  0.0 6.7 %collective-permute-start = (f32[8,128]{1,0:T(8,128)S(1)}, f32[8,128]{1,0:T(8,128)S(1)}, u32[]{:S(2)}, u32[]{:S(2)}) collective-permute-start(f32[8,128]{1,0:T(8,128)S(1)} %broadcast_in_dim.3), channel_id=1, source_target_pairs={{0,64},{2,66},{4,68},{6,70},{8,72},{10,74},{12,76},{14,78},{16,80}... | collective-permute-start | bytes 12296 | tf_op jit(solution)/shard_map/ppermute | solution.py:427
  6.7 1.0 %copy-start.3 = (f32[1024,128]{1,0:T(8,128)S(1)}, f32[1024,128]{1,0:T(8,128)}, u32[]{:S(2)}) copy-start(f32[1024,128]{1,0:T(8,128)} %x_ref.1) | copy-start | bytes 1572868
  7.8 34.3 %copy-start.4 = (bf16[4,2,256,128]{3,2,1,0:T(8,128)(2,1)S(1)}, bf16[4,2,256,128]{3,2,1,0:T(8,128)(2,1)}, u32[]{:S(2)}) copy-start(bf16[4,2,256,128]{3,2,1,0:T(8,128)(2,1)} %basis_ref.2) | copy-start | bytes 1572868
  42.1 23.7 %copy-start = (bf16[4,7,2,128,128]{4,3,2,1,0:T(8,128)(2,1)S(1)}, bf16[4,7,2,128,128]{4,3,2,1,0:T(8,128)(2,1)}, u32[]{:S(2)}) copy-start(bf16[4,7,2,128,128]{4,3,2,1,0:T(8,128)(2,1)} %couplings_ref.3) | copy-start | bytes 5505028
  42.1 23.7 %copy-start.1 = (bf16[4,2,256,256]{3,2,1,0:T(8,128)(2,1)S(1)}, bf16[4,2,256,256]{3,2,1,0:T(8,128)(2,1)}, u32[]{:S(2)}) copy-start(bf16[4,2,256,256]{3,2,1,0:T(8,128)(2,1)} %blocks_ref.1) | copy-start | bytes 3145732
  42.8 5.1 %collective-permute-start.3 = (f32[128,256]{1,0:T(8,128)S(1)}, f32[128,256]{1,0:T(8,128)S(1)}, u32[]{:S(2)}, u32[]{:S(2)}) collective-permute-start(f32[128,256]{1,0:T(8,128)S(1)} %get-tuple-element.12), channel_id=1, source_target_pairs={{0,24},{8,16},{16,8},{24,0},{32,56},{40,48},{48,40},{56,32},{64,88... | collective-permute-start | bytes 393224 | tf_op jit(solution)/shard_map/ppermute | solution.py:410
  44.3 6.5 %collective-permute-start.2 = (f32[128,256]{1,0:T(8,128)S(1)}, f32[128,256]{1,0:T(8,128)S(1)}, u32[]{:S(2)}, u32[]{:S(2)}) collective-permute-start(f32[128,256]{1,0:T(8,128)S(1)} %get-tuple-element.12), channel_id=1, source_target_pairs={{0,16},{8,24},{16,0},{24,8},{32,48},{40,56},{48,32},{56,40},{64,80... | collective-permute-start | bytes 393224 | tf_op jit(solution)/shard_map/ppermute | solution.py:410
  45.3 6.1 %collective-permute-start.1 = (f32[128,256]{1,0:T(8,128)S(1)}, f32[128,256]{1,0:T(8,128)S(1)}, u32[]{:S(2)}, u32[]{:S(2)}) collective-permute-start(f32[128,256]{1,0:T(8,128)S(1)} %get-tuple-element.12), channel_id=1, source_target_pairs={{0,8},{8,0},{16,24},{24,16},{32,40},{40,32},{48,56},{56,48},{64,72... | collective-permute-start | bytes 393224 | tf_op jit(solution)/shard_map/ppermute | solution.py:410
  51.4 8.7 %collective-permute-start.6 = (f32[128,256]{1,0:T(8,128)S(1)}, f32[128,256]{1,0:T(8,128)S(1)}, u32[]{:S(2)}, u32[]{:S(2)}) collective-permute-start(f32[128,256]{1,0:T(8,128)S(1)} %get-tuple-element.17), channel_id=1, source_target_pairs={{0,96},{8,104},{16,112},{24,120},{32,64},{40,72},{48,80},{56,88},{... | collective-permute-start | bytes 393224 | tf_op jit(solution)/shard_map/ppermute | solution.py:410
  52.9 10.5 %collective-permute-start.5 = (f32[128,256]{1,0:T(8,128)S(1)}, f32[128,256]{1,0:T(8,128)S(1)}, u32[]{:S(2)}, u32[]{:S(2)}) collective-permute-start(f32[128,256]{1,0:T(8,128)S(1)} %get-tuple-element.17), channel_id=1, source_target_pairs={{0,64},{8,72},{16,80},{24,88},{32,96},{40,104},{48,112},{56,120},{... | collective-permute-start | bytes 393224 | tf_op jit(solution)/shard_map/ppermute | solution.py:410
  53.5 10.0 %collective-permute-start.4 = (f32[128,256]{1,0:T(8,128)S(1)}, f32[128,256]{1,0:T(8,128)S(1)}, u32[]{:S(2)}, u32[]{:S(2)}) collective-permute-start(f32[128,256]{1,0:T(8,128)S(1)} %get-tuple-element.17), channel_id=1, source_target_pairs={{0,32},{8,40},{16,48},{24,56},{32,0},{40,8},{48,16},{56,24},{64,96... | collective-permute-start | bytes 393224 | tf_op jit(solution)/shard_map/ppermute | solution.py:410
  63.5 10.3 %collective-permute-start.7 = (f32[128,256]{1,0:T(8,128)S(1)}, f32[128,256]{1,0:T(8,128)S(1)}, u32[]{:S(2)}, u32[]{:S(2)}) collective-permute-start(f32[128,256]{1,0:T(8,128)S(1)} %get-tuple-element.15), channel_id=1, source_target_pairs={{0,128},{8,136},{16,144},{24,152},{32,160},{40,168},{48,176},{56,1... | collective-permute-start | bytes 393224 | tf_op jit(solution)/shard_map/ppermute | solution.py:410
  65.7 8.0 %copy-start.5 = (bf16[4,2,256,128]{3,2,1,0:T(8,128)(2,1)S(1)}, bf16[4,2,256,128]{3,2,1,0:T(8,128)(2,1)}, u32[]{:S(2)}) copy-start(bf16[4,2,256,128]{3,2,1,0:T(8,128)(2,1)} %basis_ref.3) | copy-start | bytes 1572868
  74.6 23.4 %copy-start.2 = (bf16[8,2,128,256]{3,2,1,0:T(8,128)(2,1)S(1)}, bf16[8,2,128,256]{3,2,1,0:T(8,128)(2,1)}, u32[]{:S(2)}) copy-start(bf16[8,2,128,256]{3,2,1,0:T(8,128)(2,1)} %constant.4.clone.table_ref) | copy-start | bytes 3145732
